TPU v7x, 128 devices: a whole 4x4x4 slice. The times are simulated.
128 devices in a mesh: ping: 8 (over y, x_hi), range: 8 (over z, x_lo), elev: 2 (over core).
Axes of the slice: x: 4 (x_hi: 2, x_lo: 2; x = x_hi * 2 + x_lo), y: 4, z: 4, core: 2. Of those that a mesh axis runs over, the one named last changes fastest.
Arguments:
- echoes: bfloat16 [32, 16, 64, 1024], P('ping', 'elev', None, 'range'), may hold values from -6 to 6
- steer: bfloat16 [16, 8, 1024], P('elev', None, 'range'), may hold values from -1.5 to 1.5
- offsets: int32 [32], P('ping'), may hold values from 0 to 64, as said below
- delays: int32 [32, 256], P('ping'), may hold values from 0 to 7
- aperture: int32 [128, 32], P(None, 'ping'), may hold values 0 or 1
Outputs:
- image: bfloat16 [128, 8, 1024], P(('ping', 'elev'), None, 'range')
Inputs may be any that keep to these rules, and one draw needn't show every extreme that they name: offsets[p] + 64 <= 128, so every element of every ping lies on a voxel column.
All inputs are finite; a program needn't handle non-finite values. No bound on the sum of `aperture` on one device may be relied on, other than what follows from the above.
Results may differ from a plain program's by a relative error of at most 0.0049.
Values may be sent and summed in bfloat16 or wider, within the bound.
A program may use at most 64 MiB of HBM per device.

v0:
```python
import jax
import jax.numpy as jnp
from jax import lax
from jax.sharding import PartitionSpec as P

DMAX = 8
COLS_DEV = 8


def from_behind(value, axis, steps):
    count = lax.axis_size(axis)
    leading, last = (max(0, -steps), min(count, count - steps))
    return lax.ppermute(value, axis, [(source, source + steps) for source in range(leading, last)])


def body(echoes, steer, offsets, delays, aperture):
    pings, elems, along, bins = echoes.shape
    beams_count = steer.shape[1]
    columns_all = delays.shape[1] // 2
    accum = jnp.zeros((pings, along, beams_count, bins), jnp.float32)
    for element in range(elems):
        echo_part = echoes[:, element, :, None, :].astype(jnp.float32)
        accum = accum + echo_part * steer[element][None, None].astype(jnp.float32)
    partial_value = accum.astype(jnp.bfloat16)
    head = partial_value[..., : DMAX - 1]
    after = from_behind(head, "range", -1)
    extended = jnp.concatenate([partial_value, after], axis=3)
    scale = float(lax.axis_size("ping") * pings * along) ** (-0.5)
    first = jnp.int32(0)
    per_ping = []
    for ping_pos in range(pings):
        anchor = first - offsets[ping_pos] - (along - 1) + columns_all
        window = lax.dynamic_slice_in_dim(
            delays[ping_pos], anchor, lax.axis_size(("ping", "elev")) * COLS_DEV + along - 1, 0
        )
        slides = [
            window[along - 1 - elem : along - 1 - elem + lax.axis_size(("ping", "elev")) * COLS_DEV]
            for elem in range(along)
        ]
        per_ping.append(jnp.stack(slides, axis=1))
    picked = jnp.stack(per_ping, axis=1)
    product = jnp.zeros(
        (lax.axis_size(("ping", "elev")) * COLS_DEV, beams_count * bins), jnp.float32
    )
    for shift in range(DMAX):
        count = picked.shape[0]
        weight = jnp.where(picked == shift, aperture[:, :, None], 0)
        weight = weight.astype(jnp.bfloat16).reshape(count, pings * along)
        product = product + jnp.dot(
            weight,
            extended[..., shift : shift + bins].reshape(pings * along, beams_count * bins),
            preferred_element_type=jnp.float32,
        )
    total = lax.psum_scatter(
        product.reshape(lax.axis_size(("ping", "elev")) * COLS_DEV, beams_count, bins),
        ("ping", "elev"),
        scatter_dimension=0,
        tiled=True,
    )
    return (total * scale).astype(jnp.bfloat16)


def solution(mesh):
    placed = (
        P("ping", "elev", None, "range"),
        P("elev", None, "range"),
        P("ping"),
        P("ping", None),
        P(None, "ping"),
    )
    return jax.shard_map(
        body,
        mesh=mesh,
        in_specs=placed,
        out_specs=P(("ping", "elev"), None, "range"),
        check_vma=False,
    )
```

profile of v0, /device:TPU:1, one launch (start us, length us, event | category | flops | bytes accessed | tf_op | source)
XLA Modules:
  0.0 105.0 jit_solution(6722826865813223664)
XLA Ops:
  6.5 0.8 bitcast_convert_fusion.15
  7.3 1.1 %bitcast_convert_fusion.7 = (f32[4,64,128]{2,1,0:T(8,128)S(1)}, f32[4,64,128]{2,1,0:T(8,128)S(1)}, f32[4,64,128]{2,1,0:T(8,128)S(1)}, f32[4,64,128]{2,1,0:T(8,12...) fusion(bf16[4,8,64,128]{3,2,1,0:T(8,128)(2,1)} %param.5), kind=kLoop, calls=%fused_computation.61 | loop fusion | flops 262144 | bytes 1572864 | tf_op jit(solution)/shard_map/convert_element_type | solution.py:22
  8.5 0.6 add_convert_fusion
  9.1 1.3 %collective-permute-start = (bf16[4,64,8,7]{3,2,1,0:T(8,128)(2,1)S(1)}, bf16[4,64,8,7]{3,2,1,0:T(8,128)(2,1)S(1)}, u32[]{:S(2)}, u32[]{:S(2)}) collective-permute-start(bf16[4,64,8,7]{3,2,1,0:T(8,128)(2,1)S(1)} %bitcast.632), channel_id=1, source_target_pairs={{2,0},{4,2},{6,4},{8,6},{10,8},{12,10},{14,12},{3,1},{5,3},{7,5},{... | collective-permute-start | bytes 86024 | tf_op jit(solution)/shard_map/ppermute | solution.py:13
  10.4 0.7 fusion.281
  16.5 0.7 copy-done.2
  19.5 0.2 stack.859
  19.7 0.2 stack.925
  19.8 0.2 stack.1057
  20.0 0.2 stack.991
  20.2 0.7 copy-done
  21.0 0.2 fusion.21
  21.3 2.9 %collective-permute-done = bf16[4,64,8,7]{3,2,1,0:T(8,128)(2,1)S(1)} collective-permute-done((bf16[4,64,8,7]{3,2,1,0:T(8,128)(2,1)S(1)}, bf16[4,64,8,7]{3,2,1,0:T(8,128)(2,1)S(1)}, u32[]{:S(2)}, u32[]{:S(2)}) %collective-permute-start) | collective-permute-done | bytes 28704 | tf_op jit(solution)/shard_map/ppermute | solution.py:13
  24.2 2.1 %pad_maximum_fusion = (bf16[4,64,8,128]{3,2,1,0:T(8,128)(2,1)S(1)}, bf16[4,64,8,128]{3,2,1,0:T(8,128)(2,1)S(1)}, bf16[4,64,8,128]{3,2,1,0:T(8,128)(2,1)S(1)}, bf...) fusion(bf16[4,64,8,7]{3,2,1,0:T(8,128)(2,1)S(1)} %collective-pe, ...), kind=kLoop, calls=%fused_computation.44 | loop fusion | flops 7340032 | bytes 4222976 | tf_op jit(solution)/shard_map/concatenate | solution.py:27
  26.2 0.3 convolution_add_fusion.6
  26.5 0.3 convolution_add_fusion.5
  26.8 0.3 convolution_add_fusion.4
  27.0 0.3 convolution_add_fusion.3
  27.3 0.3 convolution_add_fusion.2
  27.5 0.3 convolution_add_fusion.1
  27.8 0.3 fusion
  28.1 0.9 copy.14
  29.0 67.8 %reduce-scatter.2.cloned.1.call-done = f32[8,8,128]{2,1,0:T(8,128)} async-done(((f32[128,8,128]{2,1,0:T(8,128)}), f32[8,8,128]{2,1,0:T(8,128)}) %reduce-scatter.2.cloned.1.call-update) | async-done | bytes 32784 | tf_op jit(solution)/shard_map/reduce_scatter | solution.py:54
  96.8 1.4 %multiply_convert_fusion = bf16[8,8,128]{2,1,0:T(8,128)(2,1)} fusion(f32[8,8,128]{2,1,0:T(8,128)} %reduce-scatter.2.cloned.1.call-done), kind=kLoop, calls=%fused_computation.318 | loop fusion | flops 16384 | bytes 49152 | tf_op jit(solution)/shard_map/convert_element_type | solution.py:60
  (25 shorter events, 2.5 us)
Async XLA Ops:
  6.5 90.3 %reduce-scatter.2.cloned.1.call-start = ((), (), s32[]{:S(2)}) async-start(), calls=%async_computation.1 | async-start | bytes 557056 | tf_op jit(solution)/shard_map/reduce_scatter | solution.py:54
  9.1 1.3 %copy-start.1 = (s32[4]{0:T(128)S(1)}, s32[4]{0:T(128)}, u32[]{:S(2)}) copy-start(s32[4]{0:T(128)} %param.7) | copy-start | bytes 52
  9.1 15.1 %collective-permute-start = (bf16[4,64,8,7]{3,2,1,0:T(8,128)(2,1)S(1)}, bf16[4,64,8,7]{3,2,1,0:T(8,128)(2,1)S(1)}, u32[]{:S(2)}, u32[]{:S(2)}) collective-permute-start(bf16[4,64,8,7]{3,2,1,0:T(8,128)(2,1)S(1)} %bitcast.632), channel_id=1, source_target_pairs={{2,0},{4,2},{6,4},{8,6},{10,8},{12,10},{14,12},{3,1},{5,3},{7,5},{... | collective-permute-start | bytes 86024 | tf_op jit(solution)/shard_map/ppermute | solution.py:13
  16.5 0.7 copy-start.2
  20.2 0.7 copy-start
Sparse Core Ops, SparseCore 0:
  29.1 67.6 reduce-scatter.1
where the time goes:
time: 106 us; the launch traced here: 105 us
  waiting for transfers between devices  70.7 us (67%)
  between operations  18.9 us (18%)
  other arithmetic  6.09 us (6%)
  local copies, waits for them, and re-layouts  5.97 us (6%)
  matrix products  2.03 us (2%)
  starting transfers between devices  1.29 us (1%)
    reduce_scatter x1, waiting for transfers between devices, body(): lax.psum_scatter(product.reshape(lax.axis_size(('ping', 'elev')) * COLS_D...  67.8 us
    another operation x20, local copies, waits for them, and re-layouts, body(): per_ping.append(jnp.stack(slides, axis=1))  3.02 us
    ppermute x1, waiting for transfers between devices, from_behind(): lax.ppermute(value, axis, [(source, source + steps) for source in range(l...  2.88 us
    unnamed x7, local copies, waits for them, and re-layouts  2.27 us
  transfers between devices with their start and end apart: 2, of which 2 were waited for; matrix products, arithmetic and copies ran while one was open for 4% of the time, Pallas kernels for 0%

commit v1 on v0

v1 whole, which is shorter than its diff:
```python
import functools

import jax
import jax.numpy as jnp
from jax import lax
from jax.experimental import pallas as pl
from jax.experimental.pallas import tpu as pltpu
from jax.sharding import PartitionSpec as P

MESH = pl.DeviceIdType.MESH
DMAX = 8
F32 = jnp.float32
BF16 = jnp.bfloat16

ROUTES = ((2, 1), (2, 0), (1, 1), (3, 1), (1, 0), (3, 0), (0, 1), (0, 0))


def target_of(ping, route):
    steps, flip = route
    y, far = ping // 2, ping % 2
    return ((y + steps) % 4) * 2 + (far + flip) % 2


def lanes(shape):
    return lax.broadcasted_iota(jnp.int32, shape, len(shape) - 1)


def rows_of(shape):
    return lax.broadcasted_iota(jnp.int32, shape, len(shape) - 2)


def kernel(
    scale, groups,
    echo_hbm, steer_hbm, off_hbm, delay_hbm, ap_hbm, out_ref,
    echo, steer, off, delay, ap, spread, wide, table, weight, pick_t,
    head, halo, give, own, sib, halo_rows, stage, got,
    in_sem, small_sem, halo_send, halo_recv, sib_send, sib_recv, share_send, share_recv,
):
    ping = lax.axis_index("ping")
    rng = lax.axis_index("range")
    elev = lax.axis_index("elev")
    other = 1 - elev
    pings, elems, along, bins = echo.shape
    half = steer.shape[1] // 2
    depth = pings * along

    loads = [
        pltpu.make_async_copy(src, dst, small_sem.at[i])
        for i, (src, dst) in enumerate(
            ((steer_hbm, steer), (off_hbm, off), (delay_hbm, delay), (ap_hbm, ap))
        )
    ]
    for load in loads:
        load.start()
    echo_loads = [
        pltpu.make_async_copy(echo_hbm.at[p], echo.at[p], in_sem.at[p]) for p in range(pings)
    ]
    for load in echo_loads:
        load.start()

    below = (rng + groups - 1) % groups
    above = (rng + 1) % groups
    barrier = pltpu.get_barrier_semaphore()
    peers = []
    for route in ROUTES:
        for side in (other, elev):
            if route != (0, 0) or side is other:
                peers.append({"ping": target_of(ping, route), "elev": side})
    for group in (below, above):
        for side in (0, 1):
            peers.append({"range": group, "elev": jnp.int32(side)})
    for peer in peers:
        pl.semaphore_signal(barrier, inc=1, device_id=peer, device_id_type=MESH)

    loads[0].wait()
    wide[...] = jnp.zeros_like(wide)
    low = lanes((8, bins)) == rows_of((8, bins))
    for e in range(elems):
        rows = steer[e].astype(F32)
        for c in range(2):
            diag = jnp.zeros((8, bins), F32)
            for b in range(half):
                beam = c * half + b
                line = jnp.broadcast_to(rows[beam : beam + 1], (8, bins))
                spread[beam, e] = line
                part = jnp.where(low, line, 0.0)
                diag = diag + (pltpu.roll(part, 8 * b, 1) if b else part)
            diag = diag + pltpu.roll(diag, 32, 1)
            diag = diag + pltpu.roll(diag, 64, 1)
            both = jnp.concatenate([diag, jnp.zeros_like(diag)], axis=0).astype(BF16)
            wide[pl.ds(e * bins, 16), pl.ds(c * bins, bins)] = both

    for load in echo_loads:
        load.wait()
    lhs = jnp.concatenate(
        [jnp.concatenate([echo[p, e] for e in range(elems)], axis=1) for p in range(pings)], axis=0
    )
    first = jnp.dot(lhs, wide[...], preferred_element_type=F32)
    place = (lanes((along, 2 * bins)) // 32) % 4
    packed = first[:along]
    for p in range(1, pings):
        packed = jnp.where(place == p, first[p * along : (p + 1) * along], packed)
    packed = packed.astype(BF16)
    for c in range(2):
        head[c] = packed[:, c * bins : (c + 1) * bins]

    pl.semaphore_wait(barrier, len(peers))

    halo_copies = []
    for c in range(2):
        copy = pltpu.make_async_remote_copy(
            src_ref=head.at[c],
            dst_ref=halo.at[elev],
            send_sem=halo_send.at[c],
            recv_sem=halo_recv.at[elev],
            device_id={"range": below, "elev": jnp.int32(c)},
            device_id_type=MESH,
        )
        copy.start()
        halo_copies.append(copy)

    def beams(p, side, dst):
        def tile(i, carry):
            start = pl.multiple_of(i * 16, 16)
            values = [echo[p, e, pl.ds(start, 16), :].astype(F32) for e in range(elems)]
            for b in range(half):
                total = None
                for e in range(elems):
                    line = spread[side * half + b, e]
                    term = values[e] * jnp.concatenate([line, line], axis=0)
                    total = term if total is None else total + term
                dst[p, pl.ds(start, 16), pl.ds(b * bins, bins)] = total.astype(BF16)
            return carry

        lax.fori_loop(0, along // 16, tile, 0)

    sib_copies = []
    for p in range(pings):
        beams(p, other, give)
        copy = pltpu.make_async_remote_copy(
            src_ref=give.at[p],
            dst_ref=sib.at[p],
            send_sem=sib_send.at[p],
            recv_sem=sib_recv.at[p],
            device_id={"elev": other},
            device_id_type=MESH,
        )
        copy.start()
        sib_copies.append(copy)
    for p in range(pings):
        beams(p, elev, own)

    for load in loads[1:]:
        load.wait()
    for p in range(pings):
        line = jnp.broadcast_to(delay[p : p + 1, :], (2 * along, 2 * bins))
        turned = pltpu.roll(line, 0, 1, stride=1, stride_axis=0)
        table[p] = turned[:, bins:].astype(F32)
    for p in range(pings):
        pick_t[pl.ds(p * along, along), :] = table[p, pl.ds(off[p], along), :]
    picked = pick_t[...].T
    valid = ap[...].astype(F32)
    left = lanes((bins, bins)) < along
    masks = [
        jnp.where(left, valid[:, 2 * q : 2 * q + 1], valid[:, 2 * q + 1 : 2 * q + 2])
        for q in range(pings // 2)
    ]
    picked = jnp.where(jnp.concatenate(masks, axis=1) != 0.0, picked, -1.0)
    blocks = picked.shape[0] // 8
    delays_iota = lax.broadcasted_iota(jnp.int32, (blocks, DMAX, 8, depth), 1).astype(F32)
    chosen = jnp.where(picked.reshape(blocks, 1, 8, depth) == delays_iota, 1.0, 0.0)
    weight[...] = chosen.reshape(blocks * DMAX * 8, depth).astype(BF16)

    for c in range(2):
        halo_copies[c].wait_send()
    for h in range(2):
        pltpu.make_async_remote_copy(
            src_ref=head.at[h],
            dst_ref=halo.at[h],
            send_sem=halo_send.at[h],
            recv_sem=halo_recv.at[h],
            device_id={"range": below},
            device_id_type=MESH,
        ).wait_recv()
    inside = jnp.where(rng < groups - 1, 1.0, 0.0).astype(F32)
    which = (jnp.int32(0), jnp.int32(1))
    for slot, h in ((0, elev), (1, other)):
        values = halo[h].astype(F32) * inside
        for p in range(pings):
            moved = pltpu.roll(values, 128 - 32 * p, 1) if p else values
            halo_rows[slot, pl.ds(p * along, along), :] = moved.astype(BF16)
    for copy in sib_copies:
        copy.wait()

    rhs = jnp.concatenate(
        [
            jnp.concatenate([own[...].reshape(depth, half * bins), halo_rows[0]], axis=1),
            jnp.concatenate([sib[...].reshape(depth, half * bins), halo_rows[1]], axis=1),
        ],
        axis=0,
    )

    def shifted(values, count):
        lane = lanes(values.shape)
        return jnp.where(lane < bins - count, pltpu.roll(values, bins - count, 1), 0.0)

    share_copies = []
    for start in range(0, len(ROUTES), 2):
        pair = ROUTES[start : start + 2]
        targets = [target_of(ping, route) for route in pair]
        picks = jnp.concatenate(
            [weight[pl.ds(pl.multiple_of(t * 128, 128), 128), :] for t in targets], axis=0
        )
        prod = jnp.dot(
            jnp.concatenate([picks, picks], axis=1), rhs, preferred_element_type=F32
        ).reshape(4, DMAX, 8, (half + 1) * bins)

        def at(d, b):
            return prod[:, d, :, b * bins : (b + 1) * bins].reshape(32, bins)

        edge = jnp.zeros((32, bins), F32)
        lane = lanes((32, bins))
        for d in range(1, DMAX):
            edge = edge + jnp.where(
                lane % 8 >= 8 - d, pltpu.roll(at(d, half), 8 - d, 1), 0.0
            )
        images = []
        for b in range(half):
            level = [at(d, b) for d in range(DMAX)]
            step = 1
            while len(level) > 1:
                level = [
                    level[i] + shifted(level[i + 1], step) for i in range(0, len(level), 2)
                ]
                step *= 2
            end = jnp.where(lane >= bins - 8, pltpu.roll(edge, bins - 8 - 8 * b, 1), 0.0)
            images.append(level[0] + end)
        for k in range(4):
            route, side = pair[k // 2], k % 2
            slot = start + k // 2
            for b in range(0, half, 2):
                rows = jnp.concatenate(
                    [images[b][8 * k : 8 * k + 8], images[b + 1][8 * k : 8 * k + 8]], axis=0
                ).astype(BF16)
                stage[slot, side, pl.ds(8 * b, 16), :] = rows
        for i, route in enumerate(pair):
            slot = start + i
            for side in (other, elev):
                if route == (0, 0) and side is elev:
                    continue
                copy = pltpu.make_async_remote_copy(
                    src_ref=stage.at[slot, side],
                    dst_ref=got.at[slot, elev],
                    send_sem=share_send.at[slot, side],
                    recv_sem=share_recv.at[slot, elev],
                    device_id={"ping": targets[i], "elev": side},
                    device_id_type=MESH,
                )
                copy.start()
                share_copies.append(copy)

    mine = len(ROUTES) - 1
    got[mine, elev] = stage[mine, elev]
    for slot in range(len(ROUTES)):
        for h in (other, elev):
            if slot == mine and h is elev:
                continue
            pltpu.make_async_remote_copy(
                src_ref=stage.at[slot, h],
                dst_ref=got.at[slot, h],
                send_sem=share_send.at[slot, h],
                recv_sem=share_recv.at[slot, h],
                device_id={"elev": other},
                device_id_type=MESH,
            ).wait_recv()
    total = got[0].astype(F32)
    for slot in range(1, len(ROUTES)):
        total = total + got[slot].astype(F32)
    out_ref[...] = (total * scale).reshape(out_ref.shape)
    for copy in share_copies:
        copy.wait_send()


def solution(mesh):
    groups = mesh.shape["range"]
    ranks = mesh.shape["ping"]

    def body(echoes, steer, offsets, delays, aperture):
        pings, elems, along, bins = echoes.shape
        beams_count = steer.shape[1]
        half = beams_count // 2
        columns = aperture.shape[0]
        depth = pings * along
        scale = float(ranks * pings * along) ** (-0.5)
        out = pl.pallas_call(
            functools.partial(kernel, scale, groups),
            out_shape=jax.ShapeDtypeStruct((beams_count, 8, bins), F32),
            in_specs=[pl.BlockSpec(memory_space=pl.ANY)] * 5,
            out_specs=pl.BlockSpec(memory_space=pltpu.VMEM),
            scratch_shapes=[
                pltpu.VMEM(echoes.shape, BF16),
                pltpu.VMEM(steer.shape, BF16),
                pltpu.SMEM(offsets.shape, jnp.int32),
                pltpu.VMEM(delays.shape, jnp.int32),
                pltpu.VMEM(aperture.shape, jnp.int32),
                pltpu.VMEM((beams_count, elems, 8, bins), F32),
                pltpu.VMEM((elems * bins, 2 * bins), BF16),
                pltpu.VMEM((pings, 2 * along, bins), F32),
                pltpu.VMEM((columns * DMAX, depth), BF16),
                pltpu.VMEM((depth, columns), F32),
                pltpu.VMEM((2, along, bins), BF16),
                pltpu.VMEM((2, along, bins), BF16),
                pltpu.VMEM((pings, along, half * bins), BF16),
                pltpu.VMEM((pings, along, half * bins), BF16),
                pltpu.VMEM((pings, along, half * bins), BF16),
                pltpu.VMEM((2, depth, bins), BF16),
                pltpu.VMEM((len(ROUTES), 2, half * 8, bins), BF16),
                pltpu.VMEM((len(ROUTES), 2, half * 8, bins), BF16),
                pltpu.SemaphoreType.DMA((pings,)),
                pltpu.SemaphoreType.DMA((4,)),
                pltpu.SemaphoreType.DMA((2,)),
                pltpu.SemaphoreType.DMA((2,)),
                pltpu.SemaphoreType.DMA((pings,)),
                pltpu.SemaphoreType.DMA((pings,)),
                pltpu.SemaphoreType.DMA((len(ROUTES), 2)),
                pltpu.SemaphoreType.DMA((len(ROUTES), 2)),
            ],
            compiler_params=pltpu.CompilerParams(
                collective_id=0, has_side_effects=True, vmem_limit_bytes=40 * 2**20
            ),
            cost_estimate=pl.CostEstimate(
                flops=2 * columns * DMAX * depth * beams_count * bins,
                bytes_accessed=echoes.size * 2,
                transcendentals=0,
            ),
        )(echoes, steer, offsets, delays, aperture)
        return jnp.transpose(out, (1, 0, 2)).astype(BF16)

    placed = (
        P("ping", "elev", None, "range"),
        P("elev", None, "range"),
        P("ping"),
        P("ping", None),
        P(None, "ping"),
    )
    return jax.shard_map(
        body,
        mesh=mesh,
        in_specs=placed,
        out_specs=P(("ping", "elev"), None, "range"),
        check_vma=False,
    )
```

time: 106 us -> 19.9 us (0.19)
  waiting for transfers between devices: 70.7 us -> 0 us
  between operations: 18.9 us -> 0.05 us
  Pallas kernels: 0 us -> 17.1 us
  other arithmetic: 6.09 us -> 0.01 us
  local copies, waits for them, and re-layouts: 5.97 us -> 2.48 us
  matrix products: 2.03 us -> 0 us
  starting transfers between devices: 1.29 us -> 0 us
    reduce_scatter x1 -> x0, waiting for transfers between devices: 67.8 us -> none  [body(): lax.psum_scatter(product.reshape(lax.axis_size(('ping', 'elev')) * COLS_D...]
    pallas_call x0 -> x1, Pallas kernels: none -> 17.1 us  [body(): pl.pallas_call(functools.partial(kernel, scale, groups), out_shape=jax.Sh...]
    convert_element_type x6 -> x1, other arithmetic: 4.03 us -> 0.01 us  [body(): return jnp.transpose(out, (1, 0, 2)).astype(BF16)]
    another operation x20 -> x0, local copies, waits for them, and re-layouts: 3.02 us -> none  [body(): per_ping.append(jnp.stack(slides, axis=1))]
    ppermute x1 -> x0, waiting for transfers between devices: 2.88 us -> none  [from_behind(): lax.ppermute(value, axis, [(source, source + steps) for source in range(l...]
    concatenate x1 -> x0, other arithmetic: 2.06 us -> none  [body(): extended = jnp.concatenate([partial_value, after], axis=3)]
    dot_general x8 -> x0, matrix products: 2.03 us -> none  [body(): jnp.dot(weight, extended[..., shift:shift + bins].reshape(pings * along,...]
    ppermute x1 -> x0, starting transfers between devices: 1.29 us -> none  [from_behind(): lax.ppermute(value, axis, [(source, source + steps) for source in range(l...]
  transfers between devices with their start and end apart: 2 -> 0, of which waited for: 2 -> 0; matrix products, arithmetic and copies ran while one was open for 4% -> 0% of each run, Pallas kernels for 0% -> 0%
where the time goes in v1:
time: 19.9 us; the launch traced here: 19.7 us
  Pallas kernels  17.1 us (86%)
  local copies, waits for them, and re-layouts  2.48 us (12%)
    pallas_call x1, Pallas kernels, body(): pl.pallas_call(functools.partial(kernel, scale, groups), out_shape=jax.Sh...  17.1 us
    unnamed x9, local copies, waits for them, and re-layouts  1.87 us
    convert_element_type x1, local copies, waits for them, and re-layouts, body(): return jnp.transpose(out, (1, 0, 2)).astype(BF16)  0.61 us

profile of v1, /device:TPU:1, one launch (start us, length us, event | category | flops | bytes accessed | tf_op | source)
XLA Modules:
  0.0 19.7 jit_solution(8432532208691138336)
XLA Ops:
  0.0 0.0 copy-start.2
  0.0 0.0 copy-start.3
  0.0 0.0 copy-start.1
  0.0 0.8 %copy.6.ap_hbm = s32[128,4]{1,0:T(8,128)S(1)} copy(s32[128,4]{0,1:T(4,128)} %param.9) | data formatting | bytes 4096 | tf_op args[4]
  0.8 0.0 copy-done.2
  0.8 0.0 copy-done.3
  0.8 0.0 copy-done.1
  0.9 0.0 copy-start
  0.9 1.0 %copy-done = bf16[4,8,64,128]{3,2,1,0:T(8,128)(2,1)S(1)} copy-done((bf16[4,8,64,128]{3,2,1,0:T(8,128)(2,1)S(1)}, bf16[4,8,64,128]{3,2,1,0:T(8,128)(2,1)}, u32[]{:S(2)}) %copy-start) | copy-done | bytes 524312
  1.9 17.1 %shard_map.55 = f32[8,8,128]{2,1,0:T(8,128)S(1)} custom-call(bf16[4,8,64,128]{3,2,1,0:T(8,128)(2,1)S(1)} %copy-done, bf16[8,8,128]{2,1,0:T(8,128)(2,1)S(1)} %copy-done.1, s32[4]{0:T(128)S(1)} %copy-done.3, s32[4,256]{1,0:T(4,128)S(1)} %copy-done.2, s32[128,4]{1,0:T(8,128)S(1)} %copy.6.ap_hbm), custom_call_target="tpu_custom_call" | custom-call | flops 536870912 | bytes 524288 | tf_op jit(solution)/shard_map/pallas_call | solution.py:295
  19.1 0.6 %copy.7 = bf16[8,8,128]{2,1,0:T(8,128)(2,1)} copy(bf16[8,8,128]{2,0,1:T(8,128)(2,1)S(1)} %convert_bitcast_fusion) | data formatting | bytes 32768 | tf_op jit(solution)/shard_map/convert_element_type | solution.py:337
  (1 shorter events, 0.0 us)
Async XLA Ops:
  0.0 0.8 %copy-start.2 = (s32[4,256]{1,0:T(4,128)S(1)}, s32[4,256]{1,0:T(4,128)}, u32[]{:S(2)}) copy-start(s32[4,256]{1,0:T(4,128)} %delay_hbm.1) | copy-start | bytes 12292
  0.0 0.8 %copy-start.3 = (s32[4]{0:T(128)S(1)}, s32[4]{0:T(128)}, u32[]{:S(2)}) copy-start(s32[4]{0:T(128)} %off_hbm.1) | copy-start | bytes 52
  0.0 0.8 %copy-start.1 = (bf16[8,8,128]{2,1,0:T(8,128)(2,1)S(1)}, bf16[8,8,128]{2,1,0:T(8,128)(2,1)}, u32[]{:S(2)}) copy-start(bf16[8,8,128]{2,1,0:T(8,128)(2,1)} %steer_hbm.1) | copy-start | bytes 49156
  0.9 1.0 %copy-start = (bf16[4,8,64,128]{3,2,1,0:T(8,128)(2,1)S(1)}, bf16[4,8,64,128]{3,2,1,0:T(8,128)(2,1)}, u32[]{:S(2)}) copy-start(bf16[4,8,64,128]{3,2,1,0:T(8,128)(2,1)} %echo_hbm.1) | copy-start | bytes 1572868

commit v2 on v0

v2 whole, which is shorter than its diff:
```python
import functools

import jax
import jax.numpy as jnp
from jax import lax
from jax.experimental import pallas as pl
from jax.experimental.pallas import tpu as pltpu
from jax.sharding import PartitionSpec as P

MESH = pl.DeviceIdType.MESH
DMAX = 8
F32 = jnp.float32
BF16 = jnp.bfloat16

ROUTES = ((2, 1), (2, 0), (1, 1), (3, 1), (0, 1), (1, 0), (3, 0), (0, 0))


def target_of(ping, route):
    steps, flip = route
    y, far = ping // 2, ping % 2
    return ((y + steps) % 4) * 2 + (far + flip) % 2


def lanes(shape):
    return lax.broadcasted_iota(jnp.int32, shape, len(shape) - 1)


def kernel(
    scale, groups,
    echo_hbm, steer_hbm, off_hbm, delay_hbm, ap_hbm, out_ref,
    echo, steer, off, delay, ap, spread, table, pick_t, weight, rhs,
    stage, stage_edge, got, got_edge,
    in_sem, small_sem, share_send, share_recv, edge_send, edge_recv,
):
    ping = lax.axis_index("ping")
    rng = lax.axis_index("range")
    elev = lax.axis_index("elev")
    other = 1 - elev
    sides = (other, elev)
    pings, elems, along, bins = echo.shape
    beams = steer.shape[1]
    depth = pings * along

    loads = [
        pltpu.make_async_copy(src, dst, small_sem.at[i])
        for i, (src, dst) in enumerate(
            ((steer_hbm, steer), (delay_hbm, delay), (off_hbm, off), (ap_hbm, ap))
        )
    ]
    for load in loads:
        load.start()
    echo_loads = [
        pltpu.make_async_copy(echo_hbm.at[p], echo.at[p], in_sem.at[p]) for p in range(pings)
    ]
    for load in echo_loads:
        load.start()

    barrier = pltpu.get_barrier_semaphore()
    for route in ROUTES:
        for side in sides:
            if route != (0, 0) or side is other:
                pl.semaphore_signal(
                    barrier, inc=1, device_id_type=MESH,
                    device_id={"ping": target_of(ping, route), "elev": side},
                )

    @pl.when(rng < groups - 1)
    def _():
        for route in ROUTES:
            for side in sides:
                pl.semaphore_signal(
                    barrier, inc=1, device_id_type=MESH,
                    device_id={"ping": target_of(ping, route), "range": rng + 1, "elev": side},
                )

    for load in loads:
        load.wait()
    for p in range(pings):
        line = jnp.broadcast_to(delay[p : p + 1, :], (2 * along, 2 * bins))
        turned = pltpu.roll(line, 0, 1, stride=1, stride_axis=0)
        table[p] = turned[:, bins:].astype(F32)
    for p in range(pings):
        valid = ap[p : p + 1, :] != 0
        picked = table[p, pl.ds(off[p], along), :]
        pick_t[pl.ds(p * along, along), :] = jnp.where(valid, picked, -1.0)
    picked = pick_t[...].T
    blocks = picked.shape[0] // 8
    delays_iota = lax.broadcasted_iota(jnp.int32, (blocks, DMAX, 8, depth), 1).astype(F32)
    chosen = jnp.where(picked.reshape(blocks, 1, 8, depth) == delays_iota, 1.0, 0.0)
    weight[...] = chosen.reshape(blocks * DMAX * 8, depth).astype(BF16)

    for e in range(elems):
        rows = steer[e].astype(F32)
        for b in range(beams):
            spread[b, e] = jnp.broadcast_to(rows[b : b + 1], (8, bins))
    for load in echo_loads:
        load.wait()
    for p in range(pings):

        def tile(i, carry, p=p):
            start = pl.multiple_of(i * 16, 16)
            rows = pl.ds(pl.multiple_of(p * along + i * 16, 16), 16)
            values = [echo[p, e, pl.ds(start, 16), :].astype(F32) for e in range(elems)]
            lane = lanes((16, bins))
            heads = jnp.zeros((16, bins), F32)
            for b in range(beams):
                total = None
                for e in range(elems):
                    line = spread[b, e]
                    term = values[e] * jnp.concatenate([line, line], axis=0)
                    total = term if total is None else total + term
                rhs[rows, pl.ds(b * bins, bins)] = total.astype(BF16)
                first = jnp.where(lane < 8, total, 0.0)
                heads = heads + (pltpu.roll(first, 8 * b, 1) if b else first)
            rhs[rows, pl.ds(beams * bins, bins)] = heads.astype(BF16)
            return carry

        lax.fori_loop(0, along // 16, tile, 0)

    pl.semaphore_wait(barrier, 2 * len(ROUTES) - 1 + jnp.where(rng > 0, 2 * len(ROUTES), 0))

    def shifted(values, count):
        lane = lanes(values.shape)
        return jnp.where(lane < bins - count, pltpu.roll(values, bins - count, 1), 0.0)

    share_copies = []
    edge_copies = []
    for start in range(0, len(ROUTES), 2):
        pair = ROUTES[start : start + 2]
        targets = [target_of(ping, route) for route in pair]
        picks = jnp.concatenate(
            [weight[pl.ds(pl.multiple_of(t * 128, 128), 128), :] for t in targets], axis=0
        )

        def product(low, high):
            block = jnp.dot(
                picks, rhs[:, pl.ds(low * bins, (high - low) * bins)], preferred_element_type=F32
            )
            return block.reshape(4, DMAX, 8, (high - low) * bins)

        for b in range(0, beams, 2):
            prod = product(b, b + 2)
            images = []
            for c in range(2):
                level = [
                    prod[:, d, :, c * bins : (c + 1) * bins].reshape(32, bins) for d in range(DMAX)
                ]
                step = 1
                while len(level) > 1:
                    level = [
                        level[i] + shifted(level[i + 1], step) for i in range(0, len(level), 2)
                    ]
                    step *= 2
                images.append(level[0])
            for k in range(4):
                rows = jnp.concatenate([image[8 * k : 8 * k + 8] for image in images], axis=0)
                stage[start + k // 2, k % 2, pl.ds(8 * b, 16), :] = rows.astype(BF16)
        prod = product(beams, beams + 1)
        lane = lanes((32, bins))
        edge = jnp.zeros((32, bins), F32)
        for d in range(1, DMAX):
            part = pltpu.roll(prod[:, d].reshape(32, bins), 8 - d, 1)
            edge = edge + jnp.where(lane % 8 >= 8 - d, part, 0.0)
        for i in range(2):
            stage_edge[start + i] = edge[16 * i : 16 * i + 16].astype(BF16)

        for i, route in enumerate(pair):
            slot = start + i
            for side in sides:
                if route == (0, 0) and side is elev:
                    continue
                copy = pltpu.make_async_remote_copy(
                    src_ref=stage.at[slot, side],
                    dst_ref=got.at[slot, elev],
                    send_sem=share_send.at[slot, side],
                    recv_sem=share_recv.at[slot, elev],
                    device_id={"ping": targets[i], "elev": side},
                    device_id_type=MESH,
                )
                copy.start()
                share_copies.append(copy)

        @pl.when(rng > 0)
        def _(start=start, targets=targets):
            for i in range(2):
                slot = start + i
                for side in sides:
                    copy = pltpu.make_async_remote_copy(
                        src_ref=stage_edge.at[slot],
                        dst_ref=got_edge.at[slot, elev],
                        send_sem=edge_send.at[slot, side],
                        recv_sem=edge_recv.at[slot, elev],
                        device_id={"ping": targets[i], "range": rng - 1, "elev": side},
                        device_id_type=MESH,
                    )
                    copy.start()

    def share_of(slot, h):
        return pltpu.make_async_remote_copy(
            src_ref=stage.at[slot, h],
            dst_ref=got.at[slot, h],
            send_sem=share_send.at[slot, h],
            recv_sem=share_recv.at[slot, h],
            device_id={"elev": other},
            device_id_type=MESH,
        )

    def edge_of(slot, h):
        return pltpu.make_async_remote_copy(
            src_ref=stage_edge.at[slot],
            dst_ref=got_edge.at[slot, h],
            send_sem=edge_send.at[slot, h],
            recv_sem=edge_recv.at[slot, h],
            device_id={"elev": other},
            device_id_type=MESH,
        )

    mine = len(ROUTES) - 1
    total = stage[mine, elev].astype(F32)
    for slot in range(len(ROUTES)):
        for h in sides:
            if slot == mine and h is elev:
                continue
            share_of(slot, h).wait_recv()
            total = total + got[slot, h].astype(F32)

    @pl.when(rng < groups - 1)
    def _():
        for slot in range(len(ROUTES)):
            for h in sides:
                edge_of(slot, h).wait_recv()

    @pl.when(rng == groups - 1)
    def _():
        got_edge[...] = jnp.zeros_like(got_edge)

    edge = jnp.zeros((16, bins), F32)
    for slot in range(len(ROUTES)):
        for h in range(2):
            edge = edge + got_edge[slot, h].astype(F32)
    edge = jnp.where(elev == 0, edge[:8], edge[8:])
    lane = lanes((8, bins))
    for b in range(beams):
        end = jnp.where(lane >= bins - 8, pltpu.roll(edge, bins - 8 - 8 * b, 1), 0.0)
        out_ref[b] = (total[8 * b : 8 * b + 8] + end) * scale

    for copy in share_copies:
        copy.wait_send()

    @pl.when(rng > 0)
    def _():
        for slot in range(len(ROUTES)):
            for h in sides:
                edge_of(slot, h).wait_send()


def solution(mesh):
    groups = mesh.shape["range"]
    ranks = mesh.shape["ping"]

    def body(echoes, steer, offsets, delays, aperture):
        pings, elems, along, bins = echoes.shape
        beams = steer.shape[1]
        columns = aperture.shape[0]
        depth = pings * along
        scale = float(ranks * pings * along) ** (-0.5)
        slots = (len(ROUTES), 2)
        out = pl.pallas_call(
            functools.partial(kernel, scale, groups),
            out_shape=jax.ShapeDtypeStruct((beams, 8, bins), F32),
            in_specs=[pl.BlockSpec(memory_space=pltpu.HBM)] * 5,
            out_specs=pl.BlockSpec(memory_space=pltpu.VMEM),
            scratch_shapes=[
                pltpu.VMEM(echoes.shape, BF16),
                pltpu.VMEM(steer.shape, BF16),
                pltpu.SMEM(offsets.shape, jnp.int32),
                pltpu.VMEM(delays.shape, jnp.int32),
                pltpu.VMEM((pings, columns), jnp.int32),
                pltpu.VMEM((beams, elems, 8, bins), F32),
                pltpu.VMEM((pings, 2 * along, bins), F32),
                pltpu.VMEM((depth, columns), F32),
                pltpu.VMEM((columns * DMAX, depth), BF16),
                pltpu.VMEM((depth, (beams + 1) * bins), BF16),
                pltpu.VMEM(slots + (beams * 8, bins), BF16),
                pltpu.VMEM((len(ROUTES), 16, bins), BF16),
                pltpu.VMEM(slots + (beams * 8, bins), BF16),
                pltpu.VMEM(slots + (16, bins), BF16),
                pltpu.SemaphoreType.DMA((pings,)),
                pltpu.SemaphoreType.DMA((4,)),
                pltpu.SemaphoreType.DMA(slots),
                pltpu.SemaphoreType.DMA(slots),
                pltpu.SemaphoreType.DMA(slots),
                pltpu.SemaphoreType.DMA(slots),
            ],
            compiler_params=pltpu.CompilerParams(
                collective_id=0, has_side_effects=True, vmem_limit_bytes=60 * 2**20
            ),
            cost_estimate=pl.CostEstimate(
                flops=2 * columns * DMAX * depth * beams * bins,
                bytes_accessed=echoes.size * 2,
                transcendentals=0,
            ),
        )(echoes, steer, offsets, delays, jnp.transpose(aperture))
        return jnp.transpose(out, (1, 0, 2)).astype(BF16)

    placed = (
        P("ping", "elev", None, "range"),
        P("elev", None, "range"),
        P("ping"),
        P("ping", None),
        P(None, "ping"),
    )
    return jax.shard_map(
        body,
        mesh=mesh,
        in_specs=placed,
        out_specs=P(("ping", "elev"), None, "range"),
        check_vma=False,
    )
```

time: 106 us -> 17.1 us (0.16)
  waiting for transfers between devices: 70.7 us -> 0 us
  between operations: 18.9 us -> 0.01 us
  Pallas kernels: 0 us -> 15.5 us
  local copies, waits for them, and re-layouts: 5.97 us -> 0.61 us
  other arithmetic: 6.09 us -> 0.76 us
  matrix products: 2.03 us -> 0 us
  starting transfers between devices: 1.29 us -> 0 us
    reduce_scatter x1 -> x0, waiting for transfers between devices: 67.8 us -> none  [body(): lax.psum_scatter(product.reshape(lax.axis_size(('ping', 'elev')) * COLS_D...]
    pallas_call x0 -> x1, Pallas kernels: none -> 15.5 us  [body(): pl.pallas_call(functools.partial(kernel, scale, groups), out_shape=jax.Sh...]
    convert_element_type x6 -> x1, other arithmetic: 4.03 us -> 0.76 us  [body(): return jnp.transpose(out, (1, 0, 2)).astype(BF16)]
    another operation x20 -> x0, local copies, waits for them, and re-layouts: 3.02 us -> none  [body(): per_ping.append(jnp.stack(slides, axis=1))]
    ppermute x1 -> x0, waiting for transfers between devices: 2.88 us -> none  [from_behind(): lax.ppermute(value, axis, [(source, source + steps) for source in range(l...]
    unnamed x7 -> x0, local copies, waits for them, and re-layouts: 2.27 us -> none
    concatenate x1 -> x0, other arithmetic: 2.06 us -> none  [body(): extended = jnp.concatenate([partial_value, after], axis=3)]
    dot_general x8 -> x0, matrix products: 2.03 us -> none  [body(): jnp.dot(weight, extended[..., shift:shift + bins].reshape(pings * along,...]
  transfers between devices with their start and end apart: 2 -> 0, of which waited for: 2 -> 0; matrix products, arithmetic and copies ran while one was open for 4% -> 0% of each run, Pallas kernels for 0% -> 0%
where the time goes in v2:
time: 17.1 us; the launch traced here: 16.9 us
  Pallas kernels  15.5 us (91%)
  other arithmetic  0.76 us (4%)
  local copies, waits for them, and re-layouts  0.61 us (4%)
    pallas_call x1, Pallas kernels, body(): pl.pallas_call(functools.partial(kernel, scale, groups), out_shape=jax.Sh...  15.5 us
    convert_element_type x1, other arithmetic, body(): return jnp.transpose(out, (1, 0, 2)).astype(BF16)  0.76 us
    convert_element_type x1, local copies, waits for them, and re-layouts, body(): return jnp.transpose(out, (1, 0, 2)).astype(BF16)  0.61 us

profile of v2, /device:TPU:1, one launch (start us, length us, event | category | flops | bytes accessed | tf_op | source)
XLA Modules:
  0.0 16.9 jit_solution(13893761077798402132)
XLA Ops:
  0.0 15.5 %shard_map.55 = f32[8,8,128]{2,1,0:T(8,128)} custom-call(bf16[4,8,64,128]{3,2,1,0:T(8,128)(2,1)} %echo_hbm.1, bf16[8,8,128]{2,1,0:T(8,128)(2,1)} %steer_hbm.1, s32[4]{0:T(128)} %off_hbm.1, s32[4,256]{1,0:T(4,128)} %delay_hbm.1, s32[4,128]{1,0:T(4,128)} %bitcast.3), custom_call_target="tpu_custom_call" | custom-call | flops 536870912 | bytes 524288 | tf_op jit(solution)/shard_map/pallas_call | solution.py:268
  15.5 0.8 %convert_bitcast_fusion = bf16[8,8,128]{2,0,1:T(8,128)(2,1)S(1)} fusion(f32[8,8,128]{2,1,0:T(8,128)} %shard_map.55), kind=kLoop, calls=%fused_computation | loop fusion | flops 8192 | bytes 49152 | tf_op jit(solution)/shard_map/convert_element_type | solution.py:304
  16.3 0.6 %copy.6 = bf16[8,8,128]{2,1,0:T(8,128)(2,1)} copy(bf16[8,8,128]{2,0,1:T(8,128)(2,1)S(1)} %convert_bitcast_fusion) | data formatting | bytes 32768 | tf_op jit(solution)/shard_map/convert_element_type | solution.py:304

commit v3 on v2

v3 whole, which is shorter than its diff:
```python
import functools

import jax
import jax.numpy as jnp
from jax import lax
from jax.experimental import pallas as pl
from jax.experimental.pallas import tpu as pltpu
from jax.sharding import PartitionSpec as P

MESH = pl.DeviceIdType.MESH
DMAX = 8
F32 = jnp.float32
BF16 = jnp.bfloat16

ROUTES = ((2, 1), (2, 0), (1, 1), (3, 1), (0, 1), (1, 0), (3, 0), (0, 0))


def target_of(ping, route):
    steps, flip = route
    y, far = ping // 2, ping % 2
    return ((y + steps) % 4) * 2 + (far + flip) % 2


def lanes(shape):
    return lax.broadcasted_iota(jnp.int32, shape, len(shape) - 1)


def kernel(
    scale, groups,
    echo_hbm, steer_hbm, off_hbm, delay_hbm, ap_hbm, out_ref,
    echo, steer, off, delay, ap, spread, table, pick_t, weight, rhs, result,
    stage, stage_edge, got, got_edge,
    in_sem, small_sem, share_send, share_recv, edge_send, edge_recv,
):
    ping = lax.axis_index("ping")
    rng = lax.axis_index("range")
    elev = lax.axis_index("elev")
    other = 1 - elev
    sides = (other, elev)
    pings, elems, along, bins = echo.shape
    beams = steer.shape[1]
    depth = pings * along

    loads = [
        pltpu.make_async_copy(src, dst, small_sem.at[i])
        for i, (src, dst) in enumerate(
            ((steer_hbm, steer), (delay_hbm, delay), (off_hbm, off), (ap_hbm, ap))
        )
    ]
    for load in loads:
        load.start()
    echo_loads = [
        pltpu.make_async_copy(echo_hbm.at[p], echo.at[p], in_sem.at[p]) for p in range(pings)
    ]
    for load in echo_loads:
        load.start()

    barrier = pltpu.get_barrier_semaphore()
    for route in ROUTES:
        for side in sides:
            if route != (0, 0) or side is other:
                pl.semaphore_signal(
                    barrier, inc=1, device_id_type=MESH,
                    device_id={"ping": target_of(ping, route), "elev": side},
                )

    @pl.when(rng < groups - 1)
    def _():
        for route in ROUTES:
            for side in sides:
                pl.semaphore_signal(
                    barrier, inc=1, device_id_type=MESH,
                    device_id={"ping": target_of(ping, route), "range": rng + 1, "elev": side},
                )

    for load in loads:
        load.wait()
    for p in range(pings):
        line = jnp.broadcast_to(delay[p : p + 1, :], (2 * along, 2 * bins))
        turned = pltpu.roll(line, 0, 1, stride=1, stride_axis=0)
        table[p] = turned[:, bins:].astype(F32)
    for p in range(pings):
        valid = ap[p : p + 1, :] != 0
        picked = table[p, pl.ds(off[p], along), :]
        pick_t[pl.ds(p * along, along), :] = jnp.where(valid, picked, -1.0)
    picked = pick_t[...].T.astype(BF16)
    columns = picked.shape[0]
    one, zero = jnp.ones((), BF16), jnp.zeros((), BF16)
    for high in range(2):
        for low in range(4):
            weight[pl.ds(high * columns, columns), pl.ds(low * depth, depth)] = jnp.where(
                picked == 4 * high + low, one, zero
            )

    for e in range(elems):
        rows = steer[e].astype(F32)
        for b in range(beams):
            spread[b, e] = jnp.broadcast_to(rows[b : b + 1], (8, bins))
    for load in echo_loads:
        load.wait()

    def later(values, count):
        moved = pltpu.roll(values, bins - count, 1)
        return jnp.where(lanes(values.shape) < bins - count, moved, jnp.zeros((), values.dtype))

    lane = lanes((depth, bins))
    heads = jnp.zeros((depth, bins), BF16)
    for b in range(beams):
        rows = []
        for p in range(pings):
            total = None
            for e in range(elems):
                line = jnp.concatenate([spread[b, e]] * (along // 8), axis=0)
                term = echo[p, e].astype(F32) * line
                total = term if total is None else total + term
            rows.append(total.astype(BF16))
        beam = jnp.concatenate(rows, axis=0)
        place = pl.ds(b % 2 * bins, bins)
        rhs[b // 2, pl.ds(0, depth), place] = beam
        for low in range(1, 4):
            rhs[b // 2, pl.ds(low * depth, depth), place] = later(beam, low)
        here = (lane >= 16 * b + 8) & (lane < 16 * b + 16)
        heads = jnp.where(here, pltpu.roll(beam, 16 * b + 8, 1), heads)
        if b % 2:
            prod = jnp.dot(weight[...], rhs[b // 2], preferred_element_type=F32)
            images = [
                prod[:columns, c * bins : (c + 1) * bins]
                + later(prod[columns:, c * bins : (c + 1) * bins], 4)
                for c in range(2)
            ]
            for j in range(columns // 8):
                rows = jnp.concatenate([image[8 * j : 8 * j + 8] for image in images], axis=0)
                stage[j // 2, j % 2, pl.ds(8 * (b - 1), 16), :] = rows.astype(BF16)
    heads = [heads] + [pltpu.roll(heads, bins - low, 1) for low in range(1, 4)]
    prod = jnp.dot(weight[...], jnp.concatenate(heads, axis=0), preferred_element_type=F32)
    edge = prod[:columns] + pltpu.roll(prod[columns:], bins - 4, 1)
    for t in range(columns // 16):
        stage_edge[t] = edge[16 * t : 16 * t + 16].astype(BF16)

    pl.semaphore_wait(barrier, 2 * len(ROUTES) - 1 + jnp.where(rng > 0, 2 * len(ROUTES), 0))
    share_copies = []
    for slot, route in enumerate(ROUTES):
        target = target_of(ping, route)
        for side in sides:
            if route == (0, 0) and side is elev:
                continue
            copy = pltpu.make_async_remote_copy(
                src_ref=stage.at[target, side],
                dst_ref=got.at[slot, elev],
                send_sem=share_send.at[slot, side],
                recv_sem=share_recv.at[slot, elev],
                device_id={"ping": target, "elev": side},
                device_id_type=MESH,
            )
            copy.start()
            share_copies.append(copy)

    @pl.when(rng > 0)
    def _():
        for slot, route in enumerate(ROUTES):
            target = target_of(ping, route)
            for side in sides:
                copy = pltpu.make_async_remote_copy(
                    src_ref=stage_edge.at[target],
                    dst_ref=got_edge.at[slot, elev],
                    send_sem=edge_send.at[slot, side],
                    recv_sem=edge_recv.at[slot, elev],
                    device_id={"ping": target, "range": rng - 1, "elev": side},
                    device_id_type=MESH,
                )
                copy.start()

    def share_of(slot, h):
        return pltpu.make_async_remote_copy(
            src_ref=stage.at[slot, h],
            dst_ref=got.at[slot, h],
            send_sem=share_send.at[slot, h],
            recv_sem=share_recv.at[slot, h],
            device_id={"elev": other},
            device_id_type=MESH,
        )

    def edge_of(slot, h):
        return pltpu.make_async_remote_copy(
            src_ref=stage_edge.at[slot],
            dst_ref=got_edge.at[slot, h],
            send_sem=edge_send.at[slot, h],
            recv_sem=edge_recv.at[slot, h],
            device_id={"elev": other},
            device_id_type=MESH,
        )

    mine = len(ROUTES) - 1
    total = stage[ping, elev].astype(F32)
    for slot in range(len(ROUTES)):
        for h in sides:
            if slot == mine and h is elev:
                continue
            share_of(slot, h).wait_recv()
            total = total + got[slot, h].astype(F32)

    @pl.when(rng < groups - 1)
    def _():
        for slot in range(len(ROUTES)):
            for h in sides:
                edge_of(slot, h).wait_recv()

    @pl.when(rng == groups - 1)
    def _():
        got_edge[...] = jnp.zeros_like(got_edge)

    edge = jnp.zeros((16, bins), F32)
    for slot in range(len(ROUTES)):
        for h in range(2):
            edge = edge + got_edge[slot, h].astype(F32)
    edge = jnp.where(elev == 0, edge[:8], edge[8:])
    lane = lanes((8, bins))
    for b in range(beams):
        moved = pltpu.roll(edge, (2 * bins - 8 - 16 * b) % bins, 1)
        end = jnp.where(lane >= bins - 8, moved, 0.0)
        result[:, b, :] = (total[8 * b : 8 * b + 8] + end) * scale
    out_ref[...] = result[...].astype(BF16)

    for copy in share_copies:
        copy.wait_send()

    @pl.when(rng > 0)
    def _():
        for slot in range(len(ROUTES)):
            for h in sides:
                edge_of(slot, h).wait_send()


def solution(mesh):
    groups = mesh.shape["range"]
    ranks = mesh.shape["ping"]

    def body(echoes, steer, offsets, delays, aperture):
        pings, elems, along, bins = echoes.shape
        beams = steer.shape[1]
        columns = aperture.shape[0]
        depth = pings * along
        scale = float(ranks * pings * along) ** (-0.5)
        slots = (len(ROUTES), 2)
        return pl.pallas_call(
            functools.partial(kernel, scale, groups),
            out_shape=jax.ShapeDtypeStruct((8, beams, bins), BF16),
            in_specs=[pl.BlockSpec(memory_space=pltpu.HBM)] * 5,
            out_specs=pl.BlockSpec(memory_space=pltpu.VMEM),
            scratch_shapes=[
                pltpu.VMEM(echoes.shape, BF16),
                pltpu.VMEM(steer.shape, BF16),
                pltpu.SMEM(offsets.shape, jnp.int32),
                pltpu.VMEM(delays.shape, jnp.int32),
                pltpu.VMEM((pings, columns), jnp.int32),
                pltpu.VMEM((beams, elems, 8, bins), F32),
                pltpu.VMEM((pings, 2 * along, bins), F32),
                pltpu.VMEM((depth, columns), F32),
                pltpu.VMEM((2 * columns, 4 * depth), BF16),
                pltpu.VMEM((beams // 2, 4 * depth, 2 * bins), BF16),
                pltpu.VMEM((8, beams, bins), F32),
                pltpu.VMEM(slots + (beams * 8, bins), BF16),
                pltpu.VMEM((len(ROUTES), 16, bins), BF16),
                pltpu.VMEM(slots + (beams * 8, bins), BF16),
                pltpu.VMEM(slots + (16, bins), BF16),
                pltpu.SemaphoreType.DMA((pings,)),
                pltpu.SemaphoreType.DMA((4,)),
                pltpu.SemaphoreType.DMA(slots),
                pltpu.SemaphoreType.DMA(slots),
                pltpu.SemaphoreType.DMA(slots),
                pltpu.SemaphoreType.DMA(slots),
            ],
            compiler_params=pltpu.CompilerParams(
                collective_id=0, has_side_effects=True, vmem_limit_bytes=60 * 2**20
            ),
            cost_estimate=pl.CostEstimate(
                flops=2 * columns * DMAX * depth * beams * bins,
                bytes_accessed=echoes.size * 2,
                transcendentals=0,
            ),
        )(echoes, steer, offsets, delays, jnp.transpose(aperture))

    placed = (
        P("ping", "elev", None, "range"),
        P("elev", None, "range"),
        P("ping"),
        P("ping", None),
        P(None, "ping"),
    )
    return jax.shard_map(
        body,
        mesh=mesh,
        in_specs=placed,
        out_specs=P(("ping", "elev"), None, "range"),
        check_vma=False,
    )
```

time: 17.1 us -> 16.3 us (0.953)
  Pallas kernels: 15.5 us -> 14.7 us
  other arithmetic: 0.76 us -> 0 us
  local copies, waits for them, and re-layouts: 0.61 us -> 1.32 us
    unnamed x0 -> x1, local copies, waits for them, and re-layouts: none -> 1.32 us
    pallas_call x1, Pallas kernels: 15.5 us -> 14.7 us  [body(): pl.pallas_call(functools.partial(kernel, scale, groups), out_shape=jax.Sh...]
    convert_element_type x1 -> x0, other arithmetic: 0.76 us -> none  [body(): return jnp.transpose(out, (1, 0, 2)).astype(BF16)]
    convert_element_type x1 -> x0, local copies, waits for them, and re-layouts: 0.61 us -> none  [body(): return jnp.transpose(out, (1, 0, 2)).astype(BF16)]
where the time goes in v3:
time: 16.3 us; the launch traced here: 16 us
  Pallas kernels  14.7 us (90%)
  local copies, waits for them, and re-layouts  1.32 us (8%)
    pallas_call x1, Pallas kernels, body(): pl.pallas_call(functools.partial(kernel, scale, groups), out_shape=jax.Sh...  14.7 us
    unnamed x1, local copies, waits for them, and re-layouts  1.32 us

profile of v3, /device:TPU:1, one launch (start us, length us, event | category | flops | bytes accessed | tf_op | source)
XLA Modules:
  0.0 16.0 jit_solution(1081216441576439962)
XLA Ops:
  0.0 14.7 %shard_map.55 = bf16[8,8,128]{2,1,0:T(8,128)(2,1)} custom-call(bf16[4,8,64,128]{3,2,1,0:T(8,128)(2,1)} %echo_hbm.1, bf16[8,8,128]{2,1,0:T(8,128)(2,1)} %steer_hbm.1, s32[4]{0:T(128)} %off_hbm.1, s32[4,256]{1,0:T(4,128)} %delay_hbm.1, s32[4,128]{1,0:T(4,128)} %bitcast.1), custom_call_target="tpu_custom_call" | custom-call | flops 536870912 | bytes 524288 | tf_op jit(solution)/shard_map/pallas_call | solution.py:245
  14.7 1.3 %copy.7 = bf16[8,8,128]{2,1,0:T(8,128)(2,1)} copy(bf16[8,8,128]{2,1,0:T(8,128)(2,1)} %shard_map.55) | data formatting | bytes 32768

commit v4 on v3

--- a/solution.py
+++ b/solution.py
@@ -9,6 +9,7 @@
 
 MESH = pl.DeviceIdType.MESH
 DMAX = 8
+AHEAD = 0
 F32 = jnp.float32
 BF16 = jnp.bfloat16
 
@@ -28,7 +29,7 @@
 def kernel(
     scale, groups,
     echo_hbm, steer_hbm, off_hbm, delay_hbm, ap_hbm, out_ref,
-    echo, steer, off, delay, ap, spread, table, pick_t, weight, rhs, result,
+    echo, steer, off, delay, ap, spread, table, pick_t, weight, wide, rhs, result,
     stage, stage_edge, got, got_edge,
     in_sem, small_sem, share_send, share_recv, edge_send, edge_recv,
 ):
@@ -92,20 +93,36 @@
                 picked == 4 * high + low, one, zero
             )
 
+    wide[...] = jnp.zeros_like(wide)
+    lane = lanes((beams, bins))
+    row = lax.broadcasted_iota(jnp.int32, (beams, bins), 0)
     for e in range(elems):
         rows = steer[e].astype(F32)
         for b in range(beams):
             spread[b, e] = jnp.broadcast_to(rows[b : b + 1], (8, bins))
-    for load in echo_loads:
-        load.wait()
+        moved = pltpu.roll(jnp.where(lane < 8, rows, 0.0), 8, 1, stride=16, stride_axis=0)
+        line = jnp.sum(moved, axis=0, keepdims=True)
+        diag = jnp.where(lane % 16 - 8 == row, line, 0.0)
+        diag = jnp.concatenate([diag, jnp.zeros_like(diag)], axis=0)
+        wide[pl.ds(e * bins, 16), :] = diag.astype(BF16)
 
     def later(values, count):
         moved = pltpu.roll(values, bins - count, 1)
         return jnp.where(lanes(values.shape) < bins - count, moved, jnp.zeros((), values.dtype))
 
-    lane = lanes((depth, bins))
-    heads = jnp.zeros((depth, bins), BF16)
-    for b in range(beams):
+    for load in echo_loads:
+        load.wait()
+
+    flat = [jnp.concatenate([echo[p, e] for e in range(elems)], axis=1) for p in range(pings)]
+    heads = jnp.dot(jnp.concatenate(flat, axis=0), wide[...], preferred_element_type=F32)
+    heads = heads.astype(BF16)
+    heads = [heads] + [pltpu.roll(heads, bins - low, 1) for low in range(1, 4)]
+    prod = jnp.dot(weight[...], jnp.concatenate(heads, axis=0), preferred_element_type=F32)
+    edge = prod[:columns] + pltpu.roll(prod[columns:], bins - 4, 1)
+    for t in range(columns // 16):
+        stage_edge[t] = edge[16 * t : 16 * t + 16].astype(BF16)
+
+    def make_beam(b):
         rows = []
         for p in range(pings):
             total = None
@@ -119,63 +136,76 @@
         rhs[b // 2, pl.ds(0, depth), place] = beam
         for low in range(1, 4):
             rhs[b // 2, pl.ds(low * depth, depth), place] = later(beam, low)
-        here = (lane >= 16 * b + 8) & (lane < 16 * b + 16)
-        heads = jnp.where(here, pltpu.roll(beam, 16 * b + 8, 1), heads)
-        if b % 2:
-            prod = jnp.dot(weight[...], rhs[b // 2], preferred_element_type=F32)
-            images = [
-                prod[:columns, c * bins : (c + 1) * bins]
-                + later(prod[columns:, c * bins : (c + 1) * bins], 4)
-                for c in range(2)
-            ]
-            for j in range(columns // 8):
-                rows = jnp.concatenate([image[8 * j : 8 * j + 8] for image in images], axis=0)
-                stage[j // 2, j % 2, pl.ds(8 * (b - 1), 16), :] = rows.astype(BF16)
-    heads = [heads] + [pltpu.roll(heads, bins - low, 1) for low in range(1, 4)]
-    prod = jnp.dot(weight[...], jnp.concatenate(heads, axis=0), preferred_element_type=F32)
-    edge = prod[:columns] + pltpu.roll(prod[columns:], bins - 4, 1)
-    for t in range(columns // 16):
-        stage_edge[t] = edge[16 * t : 16 * t + 16].astype(BF16)
-
-    pl.semaphore_wait(barrier, 2 * len(ROUTES) - 1 + jnp.where(rng > 0, 2 * len(ROUTES), 0))
+
+    def project(q):
+        prod = jnp.dot(weight[...], rhs[q], preferred_element_type=F32)
+        images = [
+            prod[:columns, c * bins : (c + 1) * bins]
+            + later(prod[columns:, c * bins : (c + 1) * bins], 4)
+            for c in range(2)
+        ]
+        for j in range(columns // 8):
+            rows = jnp.concatenate([image[8 * j : 8 * j + 8] for image in images], axis=0)
+            stage[j // 2, j % 2, pl.ds(16 * q, 16), :] = rows.astype(BF16)
+
     share_copies = []
-    for slot, route in enumerate(ROUTES):
-        target = target_of(ping, route)
-        for side in sides:
-            if route == (0, 0) and side is elev:
-                continue
-            copy = pltpu.make_async_remote_copy(
-                src_ref=stage.at[target, side],
-                dst_ref=got.at[slot, elev],
-                send_sem=share_send.at[slot, side],
-                recv_sem=share_recv.at[slot, elev],
-                device_id={"ping": target, "elev": side},
-                device_id_type=MESH,
-            )
-            copy.start()
-            share_copies.append(copy)
-
-    @pl.when(rng > 0)
-    def _():
+
+    def send(q):
         for slot, route in enumerate(ROUTES):
             target = target_of(ping, route)
             for side in sides:
+                if route == (0, 0) and side is elev:
+                    continue
                 copy = pltpu.make_async_remote_copy(
-                    src_ref=stage_edge.at[target],
-                    dst_ref=got_edge.at[slot, elev],
-                    send_sem=edge_send.at[slot, side],
-                    recv_sem=edge_recv.at[slot, elev],
-                    device_id={"ping": target, "range": rng - 1, "elev": side},
+                    src_ref=stage.at[target, side, pl.ds(16 * q, 16)],
+                    dst_ref=got.at[slot, elev, pl.ds(16 * q, 16)],
+                    send_sem=share_send.at[slot, side, q],
+                    recv_sem=share_recv.at[slot, elev, q],
+                    device_id={"ping": target, "elev": side},
                     device_id_type=MESH,
                 )
                 copy.start()
-
-    def share_of(slot, h):
+                share_copies.append(copy)
+
+    for b in range(2 * AHEAD + 2):
+        make_beam(b)
+    for q in range(AHEAD):
+        project(q)
+    for q in range(AHEAD, beams // 2):
+        if q > AHEAD:
+            for b in (2 * q, 2 * q + 1):
+                make_beam(b)
+        project(q)
+        if q == AHEAD:
+            pl.semaphore_wait(
+                barrier, 2 * len(ROUTES) - 1 + jnp.where(rng > 0, 2 * len(ROUTES), 0)
+            )
+
+            @pl.when(rng > 0)
+            def _():
+                for slot, route in enumerate(ROUTES):
+                    target = target_of(ping, route)
+                    for side in sides:
+                        copy = pltpu.make_async_remote_copy(
+                            src_ref=stage_edge.at[target],
+                            dst_ref=got_edge.at[slot, elev],
+                            send_sem=edge_send.at[slot, side],
+                            recv_sem=edge_recv.at[slot, elev],
+                            device_id={"ping": target, "range": rng - 1, "elev": side},
+                            device_id_type=MESH,
+                        )
+                        copy.start()
+
+            for early in range(q):
+                send(early)
+        send(q)
+
+    def share_of(slot, h, q):
         return pltpu.make_async_remote_copy(
-            src_ref=stage.at[slot, h],
-            dst_ref=got.at[slot, h],
-            send_sem=share_send.at[slot, h],
-            recv_sem=share_recv.at[slot, h],
+            src_ref=stage.at[slot, h, pl.ds(16 * q, 16)],
+            dst_ref=got.at[slot, h, pl.ds(16 * q, 16)],
+            send_sem=share_send.at[slot, h, q],
+            recv_sem=share_recv.at[slot, h, q],
             device_id={"elev": other},
             device_id_type=MESH,
         )
@@ -190,15 +220,6 @@
             device_id_type=MESH,
         )
 
-    mine = len(ROUTES) - 1
-    total = stage[ping, elev].astype(F32)
-    for slot in range(len(ROUTES)):
-        for h in sides:
-            if slot == mine and h is elev:
-                continue
-            share_of(slot, h).wait_recv()
-            total = total + got[slot, h].astype(F32)
-
     @pl.when(rng < groups - 1)
     def _():
         for slot in range(len(ROUTES)):
@@ -214,11 +235,19 @@
         for h in range(2):
             edge = edge + got_edge[slot, h].astype(F32)
     edge = jnp.where(elev == 0, edge[:8], edge[8:])
-    lane = lanes((8, bins))
-    for b in range(beams):
-        moved = pltpu.roll(edge, (2 * bins - 8 - 16 * b) % bins, 1)
-        end = jnp.where(lane >= bins - 8, moved, 0.0)
-        result[:, b, :] = (total[8 * b : 8 * b + 8] + end) * scale
+    mine = len(ROUTES) - 1
+    for q in range(beams // 2):
+        part = pl.ds(16 * q, 16)
+        total = stage[ping, elev, part, :].astype(F32)
+        for slot in range(len(ROUTES)):
+            for h in sides:
+                if slot != mine or h is other:
+                    share_of(slot, h, q).wait_recv()
+                    total = total + got[slot, h, part, :].astype(F32)
+        for b in (2 * q, 2 * q + 1):
+            moved = pltpu.roll(edge, (2 * bins - 8 - 16 * b) % bins, 1)
+            end = jnp.where(lane >= bins - 8, moved, 0.0)
+            result[:, b, :] = (total[8 * (b % 2) : 8 * (b % 2) + 8] + end) * scale
     out_ref[...] = result[...].astype(BF16)
 
     for copy in share_copies:
@@ -242,6 +271,8 @@
         depth = pings * along
         scale = float(ranks * pings * along) ** (-0.5)
         slots = (len(ROUTES), 2)
+        operands = (echoes, steer, offsets, delays, jnp.transpose(aperture))
+        operands = [pltpu.with_memory_space_constraint(v, pltpu.HBM) for v in operands]
         return pl.pallas_call(
             functools.partial(kernel, scale, groups),
             out_shape=jax.ShapeDtypeStruct((8, beams, bins), BF16),
@@ -257,6 +288,7 @@
                 pltpu.VMEM((pings, 2 * along, bins), F32),
                 pltpu.VMEM((depth, columns), F32),
                 pltpu.VMEM((2 * columns, 4 * depth), BF16),
+                pltpu.VMEM((elems * bins, bins), BF16),
                 pltpu.VMEM((beams // 2, 4 * depth, 2 * bins), BF16),
                 pltpu.VMEM((8, beams, bins), F32),
                 pltpu.VMEM(slots + (beams * 8, bins), BF16),
@@ -265,20 +297,20 @@
                 pltpu.VMEM(slots + (16, bins), BF16),
                 pltpu.SemaphoreType.DMA((pings,)),
                 pltpu.SemaphoreType.DMA((4,)),
-                pltpu.SemaphoreType.DMA(slots),
-                pltpu.SemaphoreType.DMA(slots),
+                pltpu.SemaphoreType.DMA(slots + (beams // 2,)),
+                pltpu.SemaphoreType.DMA(slots + (beams // 2,)),
                 pltpu.SemaphoreType.DMA(slots),
                 pltpu.SemaphoreType.DMA(slots),
             ],
             compiler_params=pltpu.CompilerParams(
-                collective_id=0, has_side_effects=True, vmem_limit_bytes=60 * 2**20
+                collective_id=0, has_side_effects=True, vmem_limit_bytes=40 * 2**20
             ),
             cost_estimate=pl.CostEstimate(
                 flops=2 * columns * DMAX * depth * beams * bins,
                 bytes_accessed=echoes.size * 2,
                 transcendentals=0,
             ),
-        )(echoes, steer, offsets, delays, jnp.transpose(aperture))
+        )(*operands)
 
     placed = (
         P("ping", "elev", None, "range"),

time: 16.3 us -> 15.4 us (0.945)
  local copies, waits for them, and re-layouts: 1.32 us -> 0.61 us
    unnamed x1, local copies, waits for them, and re-layouts: 1.32 us -> 0.61 us
where the time goes in v4:
time: 15.4 us; the launch traced here: 15.3 us
  Pallas kernels  14.7 us (95%)
  local copies, waits for them, and re-layouts  0.61 us (4%)
    pallas_call x1, Pallas kernels, body(): pl.pallas_call(functools.partial(kernel, scale, groups), out_shape=jax.Sh...  14.7 us
    unnamed x1, local copies, waits for them, and re-layouts  0.61 us

profile of v4, /device:TPU:1, one launch (start us, length us, event | category | flops | bytes accessed | tf_op | source)
XLA Modules:
  0.0 15.3 jit_solution(14509826720351250684)
XLA Ops:
  0.0 14.7 %shard_map.55 = bf16[8,8,128]{2,1,0:T(8,128)(2,1)S(1)} custom-call(bf16[4,8,64,128]{3,2,1,0:T(8,128)(2,1)} %echo_hbm.1, bf16[8,8,128]{2,1,0:T(8,128)(2,1)} %steer_hbm.1, s32[4]{0:T(128)} %off_hbm.1, s32[4,256]{1,0:T(4,128)} %delay_hbm.1, s32[4,128]{1,0:T(4,128)} %bitcast.1), custom_call_target="tpu_custom_call" | custom-call | flops 536870912 | bytes 524288 | tf_op jit(solution)/shard_map/pallas_call | solution.py:276
  14.7 0.6 %copy.7 = bf16[8,8,128]{2,1,0:T(8,128)(2,1)} copy(bf16[8,8,128]{2,1,0:T(8,128)(2,1)S(1)} %shard_map.55) | data formatting | bytes 32768

commit v5 on v4

--- a/solution.py
+++ b/solution.py
@@ -9,7 +9,7 @@
 
 MESH = pl.DeviceIdType.MESH
 DMAX = 8
-AHEAD = 0
+PIECES = 2
 F32 = jnp.float32
 BF16 = jnp.bfloat16
 
@@ -31,7 +31,7 @@
     echo_hbm, steer_hbm, off_hbm, delay_hbm, ap_hbm, out_ref,
     echo, steer, off, delay, ap, spread, table, pick_t, weight, wide, rhs, result,
     stage, stage_edge, got, got_edge,
-    in_sem, small_sem, share_send, share_recv, edge_send, edge_recv,
+    small_sem, share_send, share_recv, edge_send, edge_recv,
 ):
     ping = lax.axis_index("ping")
     rng = lax.axis_index("range")
@@ -50,11 +50,8 @@
     ]
     for load in loads:
         load.start()
-    echo_loads = [
-        pltpu.make_async_copy(echo_hbm.at[p], echo.at[p], in_sem.at[p]) for p in range(pings)
-    ]
-    for load in echo_loads:
-        load.start()
+    echo_load = pltpu.make_async_copy(echo_hbm, echo, small_sem.at[4])
+    echo_load.start()
 
     barrier = pltpu.get_barrier_semaphore()
     for route in ROUTES:
@@ -110,8 +107,7 @@
         moved = pltpu.roll(values, bins - count, 1)
         return jnp.where(lanes(values.shape) < bins - count, moved, jnp.zeros((), values.dtype))
 
-    for load in echo_loads:
-        load.wait()
+    echo_load.wait()
 
     flat = [jnp.concatenate([echo[p, e] for e in range(elems)], axis=1) for p in range(pings)]
     heads = jnp.dot(jnp.concatenate(flat, axis=0), wide[...], preferred_element_type=F32)
@@ -146,118 +142,106 @@
         ]
         for j in range(columns // 8):
             rows = jnp.concatenate([image[8 * j : 8 * j + 8] for image in images], axis=0)
-            stage[j // 2, j % 2, pl.ds(16 * q, 16), :] = rows.astype(BF16)
-
-    share_copies = []
-
-    def send(q):
+            stage[j, pl.ds(16 * q, 16), :] = rows.astype(BF16)
+
+    size = beams * 8 // PIECES
+
+    def send(piece):
+        part = pl.ds(size * piece, size)
         for slot, route in enumerate(ROUTES):
             target = target_of(ping, route)
             for side in sides:
                 if route == (0, 0) and side is elev:
                     continue
-                copy = pltpu.make_async_remote_copy(
-                    src_ref=stage.at[target, side, pl.ds(16 * q, 16)],
-                    dst_ref=got.at[slot, elev, pl.ds(16 * q, 16)],
-                    send_sem=share_send.at[slot, side, q],
-                    recv_sem=share_recv.at[slot, elev, q],
+                pltpu.make_async_remote_copy(
+                    src_ref=stage.at[2 * target + side, part],
+                    dst_ref=got.at[2 * slot + elev, part],
+                    send_sem=share_send.at[piece],
+                    recv_sem=share_recv.at[piece],
                     device_id={"ping": target, "elev": side},
                     device_id_type=MESH,
-                )
-                copy.start()
-                share_copies.append(copy)
-
-    for b in range(2 * AHEAD + 2):
-        make_beam(b)
-    for q in range(AHEAD):
-        project(q)
-    for q in range(AHEAD, beams // 2):
-        if q > AHEAD:
-            for b in (2 * q, 2 * q + 1):
-                make_beam(b)
-        project(q)
-        if q == AHEAD:
+                ).start()
+
+    def send_edges():
+        for slot, route in enumerate(ROUTES):
+            target = target_of(ping, route)
+            for side in sides:
+                pltpu.make_async_remote_copy(
+                    src_ref=stage_edge.at[target],
+                    dst_ref=got_edge.at[2 * slot + elev],
+                    send_sem=edge_send,
+                    recv_sem=edge_recv,
+                    device_id={"ping": target, "range": rng - 1, "elev": side},
+                    device_id_type=MESH,
+                ).start()
+
+    per = beams // 2 // PIECES
+    for piece in range(PIECES):
+        for q in range(piece * per, piece * per + per):
+            make_beam(2 * q)
+            make_beam(2 * q + 1)
+            project(q)
+        if piece == 0:
             pl.semaphore_wait(
                 barrier, 2 * len(ROUTES) - 1 + jnp.where(rng > 0, 2 * len(ROUTES), 0)
             )
-
-            @pl.when(rng > 0)
-            def _():
-                for slot, route in enumerate(ROUTES):
-                    target = target_of(ping, route)
-                    for side in sides:
-                        copy = pltpu.make_async_remote_copy(
-                            src_ref=stage_edge.at[target],
-                            dst_ref=got_edge.at[slot, elev],
-                            send_sem=edge_send.at[slot, side],
-                            recv_sem=edge_recv.at[slot, elev],
-                            device_id={"ping": target, "range": rng - 1, "elev": side},
-                            device_id_type=MESH,
-                        )
-                        copy.start()
-
-            for early in range(q):
-                send(early)
-        send(q)
-
-    def share_of(slot, h, q):
+            pl.when(rng > 0)(send_edges)
+        send(piece)
+
+    def all_shares(piece):
+        part = pl.ds(size * piece, size)
+        every = pl.ds(0, 2 * len(ROUTES) - 1)
         return pltpu.make_async_remote_copy(
-            src_ref=stage.at[slot, h, pl.ds(16 * q, 16)],
-            dst_ref=got.at[slot, h, pl.ds(16 * q, 16)],
-            send_sem=share_send.at[slot, h, q],
-            recv_sem=share_recv.at[slot, h, q],
+            src_ref=stage.at[every, part],
+            dst_ref=got.at[every, part],
+            send_sem=share_send.at[piece],
+            recv_sem=share_recv.at[piece],
             device_id={"elev": other},
             device_id_type=MESH,
         )
 
-    def edge_of(slot, h):
-        return pltpu.make_async_remote_copy(
-            src_ref=stage_edge.at[slot],
-            dst_ref=got_edge.at[slot, h],
-            send_sem=edge_send.at[slot, h],
-            recv_sem=edge_recv.at[slot, h],
-            device_id={"elev": other},
-            device_id_type=MESH,
-        )
+    all_edges = pltpu.make_async_remote_copy(
+        src_ref=got_edge,
+        dst_ref=got_edge,
+        send_sem=edge_send,
+        recv_sem=edge_recv,
+        device_id={"elev": other},
+        device_id_type=MESH,
+    )
 
     @pl.when(rng < groups - 1)
     def _():
-        for slot in range(len(ROUTES)):
-            for h in sides:
-                edge_of(slot, h).wait_recv()
+        all_edges.wait_recv()
 
     @pl.when(rng == groups - 1)
     def _():
         got_edge[...] = jnp.zeros_like(got_edge)
 
     edge = jnp.zeros((16, bins), F32)
-    for slot in range(len(ROUTES)):
-        for h in range(2):
-            edge = edge + got_edge[slot, h].astype(F32)
+    for i in range(2 * len(ROUTES)):
+        edge = edge + got_edge[i].astype(F32)
     edge = jnp.where(elev == 0, edge[:8], edge[8:])
     mine = len(ROUTES) - 1
-    for q in range(beams // 2):
-        part = pl.ds(16 * q, 16)
-        total = stage[ping, elev, part, :].astype(F32)
-        for slot in range(len(ROUTES)):
-            for h in sides:
-                if slot != mine or h is other:
-                    share_of(slot, h, q).wait_recv()
-                    total = total + got[slot, h, part, :].astype(F32)
-        for b in (2 * q, 2 * q + 1):
+    for piece in range(PIECES):
+        all_shares(piece).wait_recv()
+        part = pl.ds(size * piece, size)
+        total = stage[2 * ping + elev, part, :].astype(F32)
+        total = total + got[2 * mine + other, part, :].astype(F32)
+        for i in range(2 * mine):
+            total = total + got[i, part, :].astype(F32)
+        for k in range(size // 8):
+            b = piece * size // 8 + k
             moved = pltpu.roll(edge, (2 * bins - 8 - 16 * b) % bins, 1)
             end = jnp.where(lane >= bins - 8, moved, 0.0)
-            result[:, b, :] = (total[8 * (b % 2) : 8 * (b % 2) + 8] + end) * scale
+            result[:, b, :] = (total[8 * k : 8 * k + 8] + end) * scale
     out_ref[...] = result[...].astype(BF16)
 
-    for copy in share_copies:
-        copy.wait_send()
+    for piece in range(PIECES):
+        all_shares(piece).wait_send()
 
     @pl.when(rng > 0)
     def _():
-        for slot in range(len(ROUTES)):
-            for h in sides:
-                edge_of(slot, h).wait_send()
+        all_edges.wait_send()
 
 
 def solution(mesh):
@@ -270,7 +254,7 @@
         columns = aperture.shape[0]
         depth = pings * along
         scale = float(ranks * pings * along) ** (-0.5)
-        slots = (len(ROUTES), 2)
+        slots = (2 * len(ROUTES),)
         operands = (echoes, steer, offsets, delays, jnp.transpose(aperture))
         operands = [pltpu.with_memory_space_constraint(v, pltpu.HBM) for v in operands]
         return pl.pallas_call(
@@ -295,12 +279,11 @@
                 pltpu.VMEM((len(ROUTES), 16, bins), BF16),
                 pltpu.VMEM(slots + (beams * 8, bins), BF16),
                 pltpu.VMEM(slots + (16, bins), BF16),
-                pltpu.SemaphoreType.DMA((pings,)),
-                pltpu.SemaphoreType.DMA((4,)),
-                pltpu.SemaphoreType.DMA(slots + (beams // 2,)),
-                pltpu.SemaphoreType.DMA(slots + (beams // 2,)),
-                pltpu.SemaphoreType.DMA(slots),
-                pltpu.SemaphoreType.DMA(slots),
+                pltpu.SemaphoreType.DMA((5,)),
+                pltpu.SemaphoreType.DMA((PIECES,)),
+                pltpu.SemaphoreType.DMA((PIECES,)),
+                pltpu.SemaphoreType.DMA,
+                pltpu.SemaphoreType.DMA,
             ],
             compiler_params=pltpu.CompilerParams(
                 collective_id=0, has_side_effects=True, vmem_limit_bytes=40 * 2**20

time: 15.4 us -> 13.7 us (0.89)
  Pallas kernels: 14.7 us -> 13 us
    pallas_call x1, Pallas kernels: 14.7 us -> 13 us  [body(): pl.pallas_call(functools.partial(kernel, scale, groups), out_shape=jax.Sh...]
where the time goes in v5:
time: 13.7 us; the launch traced here: 13.6 us
  Pallas kernels  13 us (95%)
  local copies, waits for them, and re-layouts  0.61 us (4%)
    pallas_call x1, Pallas kernels, body(): pl.pallas_call(functools.partial(kernel, scale, groups), out_shape=jax.Sh...  13 us
    unnamed x1, local copies, waits for them, and re-layouts  0.61 us

profile of v5, /device:TPU:1, one launch (start us, length us, event | category | flops | bytes accessed | tf_op | source)
XLA Modules:
  0.0 13.6 jit_solution(15481065716415972613)
XLA Ops:
  0.0 13.0 %shard_map.55 = bf16[8,8,128]{2,1,0:T(8,128)(2,1)S(1)} custom-call(bf16[4,8,64,128]{3,2,1,0:T(8,128)(2,1)} %echo_hbm.1, bf16[8,8,128]{2,1,0:T(8,128)(2,1)} %steer_hbm.1, s32[4]{0:T(128)} %off_hbm.1, s32[4,256]{1,0:T(4,128)} %delay_hbm.1, s32[4,128]{1,0:T(4,128)} %bitcast.1), custom_call_target="tpu_custom_call" | custom-call | flops 536870912 | bytes 524288 | tf_op jit(solution)/shard_map/pallas_call | solution.py:260
  13.0 0.6 %copy.7 = bf16[8,8,128]{2,1,0:T(8,128)(2,1)} copy(bf16[8,8,128]{2,1,0:T(8,128)(2,1)S(1)} %shard_map.55) | data formatting | bytes 32768

commit v6 on v5

--- a/solution.py
+++ b/solution.py
@@ -9,7 +9,7 @@
 
 MESH = pl.DeviceIdType.MESH
 DMAX = 8
-PIECES = 2
+PARTS = (32, 48, 48)
 F32 = jnp.float32
 BF16 = jnp.bfloat16
 
@@ -27,7 +27,7 @@
 
 
 def kernel(
-    scale, groups,
+    scale, groups, ranks,
     echo_hbm, steer_hbm, off_hbm, delay_hbm, ap_hbm, out_ref,
     echo, steer, off, delay, ap, spread, table, pick_t, weight, wide, rhs, result,
     stage, stage_edge, got, got_edge,
@@ -37,6 +37,7 @@
     rng = lax.axis_index("range")
     elev = lax.axis_index("elev")
     other = 1 - elev
+    mine = 2 * ping + elev
     sides = (other, elev)
     pings, elems, along, bins = echo.shape
     beams = steer.shape[1]
@@ -84,11 +85,14 @@
     picked = pick_t[...].T.astype(BF16)
     columns = picked.shape[0]
     one, zero = jnp.ones((), BF16), jnp.zeros((), BF16)
-    for high in range(2):
-        for low in range(4):
-            weight[pl.ds(high * columns, columns), pl.ds(low * depth, depth)] = jnp.where(
-                picked == 4 * high + low, one, zero
-            )
+    starts = [sum(PARTS[:i]) for i in range(len(PARTS))]
+    for start, some in zip(starts, PARTS):
+        here = picked[start : start + some]
+        for high in range(2):
+            for low in range(4):
+                weight[
+                    pl.ds(2 * start + high * some, some), pl.ds(low * depth, depth)
+                ] = jnp.where(here == 4 * high + low, one, zero)
 
     wide[...] = jnp.zeros_like(wide)
     lane = lanes((beams, bins))
@@ -112,11 +116,9 @@
     flat = [jnp.concatenate([echo[p, e] for e in range(elems)], axis=1) for p in range(pings)]
     heads = jnp.dot(jnp.concatenate(flat, axis=0), wide[...], preferred_element_type=F32)
     heads = heads.astype(BF16)
-    heads = [heads] + [pltpu.roll(heads, bins - low, 1) for low in range(1, 4)]
-    prod = jnp.dot(weight[...], jnp.concatenate(heads, axis=0), preferred_element_type=F32)
-    edge = prod[:columns] + pltpu.roll(prod[columns:], bins - 4, 1)
-    for t in range(columns // 16):
-        stage_edge[t] = edge[16 * t : 16 * t + 16].astype(BF16)
+    for low in range(4):
+        moved = pltpu.roll(heads, bins - low, 1) if low else heads
+        rhs[pl.ds(low * depth, depth), pl.ds(beams * bins, bins)] = moved
 
     def make_beam(b):
         rows = []
@@ -128,78 +130,78 @@
                 total = term if total is None else total + term
             rows.append(total.astype(BF16))
         beam = jnp.concatenate(rows, axis=0)
-        place = pl.ds(b % 2 * bins, bins)
-        rhs[b // 2, pl.ds(0, depth), place] = beam
+        place = pl.ds(b * bins, bins)
+        rhs[pl.ds(0, depth), place] = beam
         for low in range(1, 4):
-            rhs[b // 2, pl.ds(low * depth, depth), place] = later(beam, low)
-
-    def project(q):
-        prod = jnp.dot(weight[...], rhs[q], preferred_element_type=F32)
+            rhs[pl.ds(low * depth, depth), place] = later(beam, low)
+
+    def project(start, some):
+        picks = weight[pl.ds(2 * start, 2 * some), :]
+        prod = jnp.dot(picks, rhs[...], preferred_element_type=F32)
         images = [
-            prod[:columns, c * bins : (c + 1) * bins]
-            + later(prod[columns:, c * bins : (c + 1) * bins], 4)
-            for c in range(2)
+            prod[:some, b * bins : (b + 1) * bins]
+            + later(prod[some:, b * bins : (b + 1) * bins], 4)
+            for b in range(beams)
         ]
-        for j in range(columns // 8):
-            rows = jnp.concatenate([image[8 * j : 8 * j + 8] for image in images], axis=0)
-            stage[j, pl.ds(16 * q, 16), :] = rows.astype(BF16)
-
-    size = beams * 8 // PIECES
-
-    def send(piece):
-        part = pl.ds(size * piece, size)
-        for slot, route in enumerate(ROUTES):
-            target = target_of(ping, route)
-            for side in sides:
-                if route == (0, 0) and side is elev:
-                    continue
-                pltpu.make_async_remote_copy(
-                    src_ref=stage.at[2 * target + side, part],
-                    dst_ref=got.at[2 * slot + elev, part],
-                    send_sem=share_send.at[piece],
-                    recv_sem=share_recv.at[piece],
-                    device_id={"ping": target, "elev": side},
-                    device_id_type=MESH,
-                ).start()
-
-    def send_edges():
-        for slot, route in enumerate(ROUTES):
-            target = target_of(ping, route)
-            for side in sides:
-                pltpu.make_async_remote_copy(
-                    src_ref=stage_edge.at[target],
-                    dst_ref=got_edge.at[2 * slot + elev],
-                    send_sem=edge_send,
-                    recv_sem=edge_recv,
-                    device_id={"ping": target, "range": rng - 1, "elev": side},
-                    device_id_type=MESH,
-                ).start()
-
-    per = beams // 2 // PIECES
-    for piece in range(PIECES):
-        for q in range(piece * per, piece * per + per):
-            make_beam(2 * q)
-            make_beam(2 * q + 1)
-            project(q)
-        if piece == 0:
+        edge = prod[:some, beams * bins :] + pltpu.roll(prod[some:, beams * bins :], bins - 4, 1)
+        for j in range(some // 8):
+            for b in range(0, beams, 2):
+                rows = [image[8 * j : 8 * j + 8] for image in images[b : b + 2]]
+                block = start // 8 + j
+                stage[block, pl.ds(8 * b, 16), :] = jnp.concatenate(rows, axis=0).astype(BF16)
+        for i in range(some // 16):
+            stage_edge[start // 16 + i] = edge[16 * i : 16 * i + 16].astype(BF16)
+
+    def send_share(target, core):
+        share = pltpu.make_async_remote_copy(
+            src_ref=stage.at[2 * target + core],
+            dst_ref=got.at[mine],
+            send_sem=share_send,
+            recv_sem=share_recv,
+            device_id={"ping": jnp.int32(target), "elev": core},
+            device_id_type=MESH,
+        )
+        if core is elev:
+            pl.when(ping != target)(share.start)
+        else:
+            share.start()
+
+    def send_edges(target):
+        for core in sides:
+            pltpu.make_async_remote_copy(
+                src_ref=stage_edge.at[target],
+                dst_ref=got_edge.at[mine],
+                send_sem=edge_send,
+                recv_sem=edge_recv,
+                device_id={"ping": jnp.int32(target), "range": rng - 1, "elev": core},
+                device_id_type=MESH,
+            ).start()
+
+    def send(start, some):
+        for target in range(start // 16, (start + some) // 16):
+            for core in sides:
+                send_share(target, core)
+            pl.when(rng > 0)(functools.partial(send_edges, target))
+
+    for b in range(beams):
+        make_beam(b)
+    for start, some in zip(starts, PARTS):
+        project(start, some)
+        if start == 0:
             pl.semaphore_wait(
                 barrier, 2 * len(ROUTES) - 1 + jnp.where(rng > 0, 2 * len(ROUTES), 0)
             )
-            pl.when(rng > 0)(send_edges)
-        send(piece)
-
-    def all_shares(piece):
-        part = pl.ds(size * piece, size)
-        every = pl.ds(0, 2 * len(ROUTES) - 1)
-        return pltpu.make_async_remote_copy(
-            src_ref=stage.at[every, part],
-            dst_ref=got.at[every, part],
-            send_sem=share_send.at[piece],
-            recv_sem=share_recv.at[piece],
-            device_id={"elev": other},
-            device_id_type=MESH,
-        )
-
+        send(start, some)
+
+    every = pl.ds(0, 2 * ranks - 1)
+    all_shares = pltpu.make_async_remote_copy(
+        src_ref=stage.at[every],
+        dst_ref=got.at[every],
+        send_sem=share_send,
+        recv_sem=share_recv,
+        device_id={"elev": other},
+        device_id_type=MESH,
+    )
     all_edges = pltpu.make_async_remote_copy(
         src_ref=got_edge,
         dst_ref=got_edge,
@@ -221,23 +223,18 @@
     for i in range(2 * len(ROUTES)):
         edge = edge + got_edge[i].astype(F32)
     edge = jnp.where(elev == 0, edge[:8], edge[8:])
-    mine = len(ROUTES) - 1
-    for piece in range(PIECES):
-        all_shares(piece).wait_recv()
-        part = pl.ds(size * piece, size)
-        total = stage[2 * ping + elev, part, :].astype(F32)
-        total = total + got[2 * mine + other, part, :].astype(F32)
-        for i in range(2 * mine):
-            total = total + got[i, part, :].astype(F32)
-        for k in range(size // 8):
-            b = piece * size // 8 + k
-            moved = pltpu.roll(edge, (2 * bins - 8 - 16 * b) % bins, 1)
-            end = jnp.where(lane >= bins - 8, moved, 0.0)
-            result[:, b, :] = (total[8 * k : 8 * k + 8] + end) * scale
+    got[mine] = stage[mine]
+    all_shares.wait_recv()
+    total = jnp.zeros((beams * 8, bins), F32)
+    for i in range(2 * ranks):
+        total = total + got[i].astype(F32)
+    for b in range(beams):
+        moved = pltpu.roll(edge, (2 * bins - 8 - 16 * b) % bins, 1)
+        end = jnp.where(lane >= bins - 8, moved, 0.0)
+        result[:, b, :] = (total[8 * b : 8 * b + 8] + end) * scale
     out_ref[...] = result[...].astype(BF16)
 
-    for piece in range(PIECES):
-        all_shares(piece).wait_send()
+    all_shares.wait_send()
 
     @pl.when(rng > 0)
     def _():
@@ -258,7 +255,7 @@
         operands = (echoes, steer, offsets, delays, jnp.transpose(aperture))
         operands = [pltpu.with_memory_space_constraint(v, pltpu.HBM) for v in operands]
         return pl.pallas_call(
-            functools.partial(kernel, scale, groups),
+            functools.partial(kernel, scale, groups, ranks),
             out_shape=jax.ShapeDtypeStruct((8, beams, bins), BF16),
             in_specs=[pl.BlockSpec(memory_space=pltpu.HBM)] * 5,
             out_specs=pl.BlockSpec(memory_space=pltpu.VMEM),
@@ -273,15 +270,15 @@
                 pltpu.VMEM((depth, columns), F32),
                 pltpu.VMEM((2 * columns, 4 * depth), BF16),
                 pltpu.VMEM((elems * bins, bins), BF16),
-                pltpu.VMEM((beams // 2, 4 * depth, 2 * bins), BF16),
+                pltpu.VMEM((4 * depth, (beams + 1) * bins), BF16),
                 pltpu.VMEM((8, beams, bins), F32),
                 pltpu.VMEM(slots + (beams * 8, bins), BF16),
                 pltpu.VMEM((len(ROUTES), 16, bins), BF16),
                 pltpu.VMEM(slots + (beams * 8, bins), BF16),
                 pltpu.VMEM(slots + (16, bins), BF16),
                 pltpu.SemaphoreType.DMA((5,)),
-                pltpu.SemaphoreType.DMA((PIECES,)),
-                pltpu.SemaphoreType.DMA((PIECES,)),
+                pltpu.SemaphoreType.DMA,
+                pltpu.SemaphoreType.DMA,
                 pltpu.SemaphoreType.DMA,
                 pltpu.SemaphoreType.DMA,
             ],

time: 13.7 us -> 12.9 us (0.942)
  the two profiles are of different devices: /device:TPU:1 before, /device:TPU:26 now
where the time goes in v6:
time: 12.9 us; the launch traced here: 12.8 us
  Pallas kernels  12.2 us (95%)
  local copies, waits for them, and re-layouts  0.61 us (5%)
    pallas_call x1, Pallas kernels, body(): pl.pallas_call(functools.partial(kernel, scale, groups, ranks), out_shape...  12.2 us
    unnamed x1, local copies, waits for them, and re-layouts  0.61 us

profile of v6, /device:TPU:26, one launch (start us, length us, event | category | flops | bytes accessed | tf_op | source)
XLA Modules:
  0.0 12.8 jit_solution(11261056917193785153)
XLA Ops:
  0.0 12.2 %shard_map.55 = bf16[8,8,128]{2,1,0:T(8,128)(2,1)S(1)} custom-call(bf16[4,8,64,128]{3,2,1,0:T(8,128)(2,1)} %echo_hbm.1, bf16[8,8,128]{2,1,0:T(8,128)(2,1)} %steer_hbm.1, s32[4]{0:T(128)} %off_hbm.1, s32[4,256]{1,0:T(4,128)} %delay_hbm.1, s32[4,128]{1,0:T(4,128)} %bitcast.1), custom_call_target="tpu_custom_call" | custom-call | flops 536870912 | bytes 524288 | tf_op jit(solution)/shard_map/pallas_call | solution.py:257
  12.2 0.6 %copy.7 = bf16[8,8,128]{2,1,0:T(8,128)(2,1)} copy(bf16[8,8,128]{2,1,0:T(8,128)(2,1)S(1)} %shard_map.55) | data formatting | bytes 32768

commit v7 on v6

--- a/solution.py
+++ b/solution.py
@@ -9,7 +9,7 @@
 
 MESH = pl.DeviceIdType.MESH
 DMAX = 8
-PARTS = (32, 48, 48)
+PARTS = (32, 96)
 F32 = jnp.float32
 BF16 = jnp.bfloat16
 
@@ -30,14 +30,13 @@
     scale, groups, ranks,
     echo_hbm, steer_hbm, off_hbm, delay_hbm, ap_hbm, out_ref,
     echo, steer, off, delay, ap, spread, table, pick_t, weight, wide, rhs, result,
-    stage, stage_edge, got, got_edge,
-    small_sem, share_send, share_recv, edge_send, edge_recv,
+    stage, swapped, summed, got, got_edge,
+    small_sem, share_send, share_recv, edge_send, edge_recv, swap_send, swap_recv,
 ):
     ping = lax.axis_index("ping")
     rng = lax.axis_index("range")
     elev = lax.axis_index("elev")
     other = 1 - elev
-    mine = 2 * ping + elev
     sides = (other, elev)
     pings, elems, along, bins = echo.shape
     beams = steer.shape[1]
@@ -55,22 +54,21 @@
     echo_load.start()
 
     barrier = pltpu.get_barrier_semaphore()
-    for route in ROUTES:
-        for side in sides:
-            if route != (0, 0) or side is other:
-                pl.semaphore_signal(
-                    barrier, inc=1, device_id_type=MESH,
-                    device_id={"ping": target_of(ping, route), "elev": side},
-                )
+    pl.semaphore_signal(
+        barrier, inc=1, device_id={"elev": other}, device_id_type=MESH
+    )
+    for route in ROUTES[:-1]:
+        pl.semaphore_signal(
+            barrier, inc=1, device_id={"ping": target_of(ping, route)}, device_id_type=MESH
+        )
 
     @pl.when(rng < groups - 1)
     def _():
         for route in ROUTES:
-            for side in sides:
-                pl.semaphore_signal(
-                    barrier, inc=1, device_id_type=MESH,
-                    device_id={"ping": target_of(ping, route), "range": rng + 1, "elev": side},
-                )
+            pl.semaphore_signal(
+                barrier, inc=1, device_id_type=MESH,
+                device_id={"ping": target_of(ping, route), "range": rng + 1},
+            )
 
     for load in loads:
         load.wait()
@@ -113,12 +111,32 @@
 
     echo_load.wait()
 
+    store = {}
+
+    class Put:
+        def __init__(self, key):
+            self.key = key
+
+        def __setitem__(self, _, value):
+            store[self.key] = value
+
+    def RHS(b, low):
+        return Put((b, low))
+
+    def PAIR(q):
+        return jnp.concatenate([jnp.concatenate([store[2*q,l] for l in range(4)],axis=0), jnp.concatenate([store[2*q+1,l] for l in range(4)],axis=0)],axis=1)
+
+    def HEADS():
+        return jnp.concatenate([store[beams,l] for l in range(4)],axis=0)
+
     flat = [jnp.concatenate([echo[p, e] for e in range(elems)], axis=1) for p in range(pings)]
-    heads = jnp.dot(jnp.concatenate(flat, axis=0), wide[...], preferred_element_type=F32)
-    heads = heads.astype(BF16)
-    for low in range(4):
-        moved = pltpu.roll(heads, bins - low, 1) if low else heads
-        rhs[pl.ds(low * depth, depth), pl.ds(beams * bins, bins)] = moved
+    flat = jnp.concatenate(flat, axis=0)
+
+    def make_heads():
+        heads = jnp.dot(flat, wide[...], preferred_element_type=F32).astype(BF16)
+        for low in range(4):
+            moved = pltpu.roll(heads, bins - low, 1) if low else heads
+            RHS(beams, low)[...] = moved
 
     def make_beam(b):
         rows = []
@@ -130,72 +148,87 @@
                 total = term if total is None else total + term
             rows.append(total.astype(BF16))
         beam = jnp.concatenate(rows, axis=0)
-        place = pl.ds(b * bins, bins)
-        rhs[pl.ds(0, depth), place] = beam
+        RHS(b, 0)[...] = beam
         for low in range(1, 4):
-            rhs[pl.ds(low * depth, depth), place] = later(beam, low)
-
-    def project(start, some):
+            RHS(b, low)[...] = later(beam, low)
+
+    def project(start, some, b):
         picks = weight[pl.ds(2 * start, 2 * some), :]
-        prod = jnp.dot(picks, rhs[...], preferred_element_type=F32)
+        prod = jnp.dot(picks, PAIR(b // 2), preferred_element_type=F32)
         images = [
-            prod[:some, b * bins : (b + 1) * bins]
-            + later(prod[some:, b * bins : (b + 1) * bins], 4)
-            for b in range(beams)
+            prod[:some, c * bins : (c + 1) * bins]
+            + later(prod[some:, c * bins : (c + 1) * bins], 4)
+            for c in range(2)
         ]
-        edge = prod[:some, beams * bins :] + pltpu.roll(prod[some:, beams * bins :], bins - 4, 1)
         for j in range(some // 8):
-            for b in range(0, beams, 2):
-                rows = [image[8 * j : 8 * j + 8] for image in images[b : b + 2]]
-                block = start // 8 + j
-                stage[block, pl.ds(8 * b, 16), :] = jnp.concatenate(rows, axis=0).astype(BF16)
+            rows = [image[8 * j : 8 * j + 8] for image in images]
+            stage[start // 16 + j // 2, j % 2, pl.ds(8 * b, 16), :] = jnp.concatenate(rows, axis=0).astype(BF16)
+
+    def project_edge(start, some):
+        picks = weight[pl.ds(2 * start, 2 * some), :]
+        prod = jnp.dot(picks, HEADS(), preferred_element_type=F32)
+        edge = prod[:some] + pltpu.roll(prod[some:], bins - 4, 1)
         for i in range(some // 16):
-            stage_edge[start // 16 + i] = edge[16 * i : 16 * i + 16].astype(BF16)
-
-    def send_share(target, core):
-        share = pltpu.make_async_remote_copy(
-            src_ref=stage.at[2 * target + core],
-            dst_ref=got.at[mine],
-            send_sem=share_send,
-            recv_sem=share_recv,
-            device_id={"ping": jnp.int32(target), "elev": core},
+            for c in range(2):
+                rows = edge[16 * i + 8 * c : 16 * i + 8 * c + 8]
+                rows = jnp.concatenate([rows, jnp.zeros_like(rows)], axis=0).astype(BF16)
+                stage[start // 16 + i, c, pl.ds(8 * beams, 16), :] = rows
+
+    def swap_of(part):
+        places = pl.ds(starts[part] // 16, PARTS[part] // 16)
+        return pltpu.make_async_remote_copy(
+            src_ref=stage.at[places, other],
+            dst_ref=swapped.at[places],
+            send_sem=swap_send.at[part],
+            recv_sem=swap_recv.at[part],
+            device_id={"elev": other},
             device_id_type=MESH,
         )
-        if core is elev:
+
+    def combine(part):
+        for target in range(starts[part] // 16, (starts[part] + PARTS[part]) // 16):
+            both = stage[target, elev].astype(F32) + swapped[target].astype(F32)
+            summed[target] = both.astype(BF16)
+
+    def send(part):
+        for target in range(starts[part] // 16, (starts[part] + PARTS[part]) // 16):
+            share = pltpu.make_async_remote_copy(
+                src_ref=summed.at[target, pl.ds(0, 8 * beams)],
+                dst_ref=got.at[ping],
+                send_sem=share_send,
+                recv_sem=share_recv,
+                device_id={"ping": jnp.int32(target)},
+                device_id_type=MESH,
+            )
             pl.when(ping != target)(share.start)
-        else:
-            share.start()
-
-    def send_edges(target):
-        for core in sides:
-            pltpu.make_async_remote_copy(
-                src_ref=stage_edge.at[target],
-                dst_ref=got_edge.at[mine],
+            edge = pltpu.make_async_remote_copy(
+                src_ref=summed.at[target, pl.ds(8 * beams, 16)],
+                dst_ref=got_edge.at[ping],
                 send_sem=edge_send,
                 recv_sem=edge_recv,
-                device_id={"ping": jnp.int32(target), "range": rng - 1, "elev": core},
+                device_id={"ping": jnp.int32(target), "range": rng - 1},
                 device_id_type=MESH,
-            ).start()
-
-    def send(start, some):
-        for target in range(start // 16, (start + some) // 16):
-            for core in sides:
-                send_share(target, core)
-            pl.when(rng > 0)(functools.partial(send_edges, target))
-
+            )
+            pl.when(rng > 0)(edge.start)
+
+    make_heads()
     for b in range(beams):
         make_beam(b)
-    for start, some in zip(starts, PARTS):
-        project(start, some)
-        if start == 0:
-            pl.semaphore_wait(
-                barrier, 2 * len(ROUTES) - 1 + jnp.where(rng > 0, 2 * len(ROUTES), 0)
-            )
-        send(start, some)
-
-    every = pl.ds(0, 2 * ranks - 1)
+    for part, (start, some) in enumerate(zip(starts, PARTS)):
+        for b in range(0, beams, 2):
+            project(start, some, b)
+        project_edge(start, some)
+        if part == 0:
+            pl.semaphore_wait(barrier, ranks + jnp.where(rng > 0, ranks, 0))
+        swap_of(part).start()
+    for part in range(len(PARTS)):
+        swap_of(part).wait_recv()
+        combine(part)
+        send(part)
+
+    every = pl.ds(0, ranks - 1)
     all_shares = pltpu.make_async_remote_copy(
-        src_ref=stage.at[every],
+        src_ref=got.at[every],
         dst_ref=got.at[every],
         send_sem=share_send,
         recv_sem=share_recv,
@@ -220,13 +253,13 @@
         got_edge[...] = jnp.zeros_like(got_edge)
 
     edge = jnp.zeros((16, bins), F32)
-    for i in range(2 * len(ROUTES)):
+    for i in range(ranks):
         edge = edge + got_edge[i].astype(F32)
-    edge = jnp.where(elev == 0, edge[:8], edge[8:])
-    got[mine] = stage[mine]
+    edge = edge[:8]
+    got[ping] = summed[ping, pl.ds(0, 8 * beams), :]
     all_shares.wait_recv()
     total = jnp.zeros((beams * 8, bins), F32)
-    for i in range(2 * ranks):
+    for i in range(ranks):
         total = total + got[i].astype(F32)
     for b in range(beams):
         moved = pltpu.roll(edge, (2 * bins - 8 - 16 * b) % bins, 1)
@@ -235,6 +268,8 @@
     out_ref[...] = result[...].astype(BF16)
 
     all_shares.wait_send()
+    for part in range(len(PARTS)):
+        swap_of(part).wait_send()
 
     @pl.when(rng > 0)
     def _():
@@ -251,7 +286,6 @@
         columns = aperture.shape[0]
         depth = pings * along
         scale = float(ranks * pings * along) ** (-0.5)
-        slots = (2 * len(ROUTES),)
         operands = (echoes, steer, offsets, delays, jnp.transpose(aperture))
         operands = [pltpu.with_memory_space_constraint(v, pltpu.HBM) for v in operands]
         return pl.pallas_call(
@@ -272,15 +306,18 @@
                 pltpu.VMEM((elems * bins, bins), BF16),
                 pltpu.VMEM((4 * depth, (beams + 1) * bins), BF16),
                 pltpu.VMEM((8, beams, bins), F32),
-                pltpu.VMEM(slots + (beams * 8, bins), BF16),
-                pltpu.VMEM((len(ROUTES), 16, bins), BF16),
-                pltpu.VMEM(slots + (beams * 8, bins), BF16),
-                pltpu.VMEM(slots + (16, bins), BF16),
+                pltpu.VMEM((ranks, 2, beams * 8 + 16, bins), BF16),
+                pltpu.VMEM((ranks, beams * 8 + 16, bins), BF16),
+                pltpu.VMEM((ranks, beams * 8 + 16, bins), BF16),
+                pltpu.VMEM((ranks, beams * 8, bins), BF16),
+                pltpu.VMEM((ranks, 16, bins), BF16),
                 pltpu.SemaphoreType.DMA((5,)),
                 pltpu.SemaphoreType.DMA,
                 pltpu.SemaphoreType.DMA,
                 pltpu.SemaphoreType.DMA,
                 pltpu.SemaphoreType.DMA,
+                pltpu.SemaphoreType.DMA((len(PARTS),)),
+                pltpu.SemaphoreType.DMA((len(PARTS),)),
             ],
             compiler_params=pltpu.CompilerParams(
                 collective_id=0, has_side_effects=True, vmem_limit_bytes=40 * 2**20

time: 12.9 us -> 12.9 us (level)
  the two profiles are of different devices: /device:TPU:26 before, /device:TPU:1 now
where the time goes in v7:
time: 12.9 us; the launch traced here: 12.8 us
  Pallas kernels  12.1 us (94%)
  local copies, waits for them, and re-layouts  0.61 us (5%)
    pallas_call x1, Pallas kernels, body(): pl.pallas_call(functools.partial(kernel, scale, groups, ranks), out_shape...  12.1 us
    unnamed x1, local copies, waits for them, and re-layouts  0.61 us

profile of v7, /device:TPU:1, one launch (start us, length us, event | category | flops | bytes accessed | tf_op | source)
XLA Modules:
  0.0 12.8 jit_solution(11101431613961028851)
XLA Ops:
  0.0 12.1 %shard_map.55 = bf16[8,8,128]{2,1,0:T(8,128)(2,1)S(1)} custom-call(bf16[4,8,64,128]{3,2,1,0:T(8,128)(2,1)} %echo_hbm.1, bf16[8,8,128]{2,1,0:T(8,128)(2,1)} %steer_hbm.1, s32[4]{0:T(128)} %off_hbm.1, s32[4,256]{1,0:T(4,128)} %delay_hbm.1, s32[4,128]{1,0:T(4,128)} %bitcast.1), custom_call_target="tpu_custom_call" | custom-call | flops 536870912 | bytes 524288 | tf_op jit(solution)/shard_map/pallas_call | solution.py:291
  12.2 0.6 %copy.7 = bf16[8,8,128]{2,1,0:T(8,128)(2,1)} copy(bf16[8,8,128]{2,1,0:T(8,128)(2,1)S(1)} %shard_map.55) | data formatting | bytes 32768

commit v8 on v7

--- a/solution.py
+++ b/solution.py
@@ -9,7 +9,8 @@
 
 MESH = pl.DeviceIdType.MESH
 DMAX = 8
-PARTS = (32, 96)
+DIRECT = 3
+PARTS = (128,)
 F32 = jnp.float32
 BF16 = jnp.bfloat16
 
@@ -62,12 +63,28 @@
             barrier, inc=1, device_id={"ping": target_of(ping, route)}, device_id_type=MESH
         )
 
+    @pl.when(ping < DIRECT)
+    def _():
+        for route in ROUTES[:-1]:
+            pl.semaphore_signal(
+                barrier, inc=1, device_id_type=MESH,
+                device_id={"ping": target_of(ping, route), "elev": other},
+            )
+
     @pl.when(rng < groups - 1)
     def _():
         for route in ROUTES:
             pl.semaphore_signal(
                 barrier, inc=1, device_id_type=MESH,
                 device_id={"ping": target_of(ping, route), "range": rng + 1},
+            )
+
+    @pl.when((rng < groups - 1) & (ping < DIRECT))
+    def _():
+        for route in ROUTES:
+            pl.semaphore_signal(
+                barrier, inc=1, device_id_type=MESH,
+                device_id={"ping": target_of(ping, route), "range": rng + 1, "elev": other},
             )
 
     for load in loads:
@@ -174,106 +191,126 @@
                 rows = jnp.concatenate([rows, jnp.zeros_like(rows)], axis=0).astype(BF16)
                 stage[start // 16 + i, c, pl.ds(8 * beams, 16), :] = rows
 
-    def swap_of(part):
-        places = pl.ds(starts[part] // 16, PARTS[part] // 16)
+    rest = pl.ds(DIRECT, ranks - DIRECT)
+    swap = pltpu.make_async_remote_copy(
+        src_ref=stage.at[rest, other],
+        dst_ref=swapped.at[rest],
+        send_sem=swap_send,
+        recv_sem=swap_recv,
+        device_id={"elev": other},
+        device_id_type=MESH,
+    )
+
+    def share(source, slot, target, core):
         return pltpu.make_async_remote_copy(
-            src_ref=stage.at[places, other],
-            dst_ref=swapped.at[places],
-            send_sem=swap_send.at[part],
-            recv_sem=swap_recv.at[part],
-            device_id={"elev": other},
+            src_ref=source.at[pl.ds(0, 8 * beams)],
+            dst_ref=got.at[slot],
+            send_sem=share_send,
+            recv_sem=share_recv,
+            device_id={"ping": jnp.int32(target), "elev": core},
             device_id_type=MESH,
         )
 
-    def combine(part):
-        for target in range(starts[part] // 16, (starts[part] + PARTS[part]) // 16):
+    def spill(source, slot, target, core):
+        return pltpu.make_async_remote_copy(
+            src_ref=source.at[pl.ds(8 * beams, 16)],
+            dst_ref=got_edge.at[slot],
+            send_sem=edge_send,
+            recv_sem=edge_recv,
+            device_id={"ping": jnp.int32(target), "range": rng - 1, "elev": core},
+            device_id_type=MESH,
+        )
+
+    def send_direct():
+        slot = 2 * ping + elev
+        for target in range(DIRECT):
+            share(stage.at[target, other], slot, target, other).start()
+            pl.when(ping != target)(share(stage.at[target, elev], slot, target, elev).start)
+
+        @pl.when(rng > 0)
+        def _():
+            for target in range(DIRECT):
+                for core in sides:
+                    spill(stage.at[target, core], slot, target, core).start()
+
+    def send_summed():
+        for target in range(DIRECT):
+            summed[target] = stage[target, elev]
+        for target in range(DIRECT, ranks):
             both = stage[target, elev].astype(F32) + swapped[target].astype(F32)
             summed[target] = both.astype(BF16)
-
-    def send(part):
-        for target in range(starts[part] // 16, (starts[part] + PARTS[part]) // 16):
-            share = pltpu.make_async_remote_copy(
-                src_ref=summed.at[target, pl.ds(0, 8 * beams)],
-                dst_ref=got.at[ping],
-                send_sem=share_send,
-                recv_sem=share_recv,
-                device_id={"ping": jnp.int32(target)},
-                device_id_type=MESH,
-            )
-            pl.when(ping != target)(share.start)
-            edge = pltpu.make_async_remote_copy(
-                src_ref=summed.at[target, pl.ds(8 * beams, 16)],
-                dst_ref=got_edge.at[ping],
-                send_sem=edge_send,
-                recv_sem=edge_recv,
-                device_id={"ping": jnp.int32(target), "range": rng - 1},
-                device_id_type=MESH,
-            )
-            pl.when(rng > 0)(edge.start)
+        for target in range(DIRECT, ranks):
+            pl.when(ping != target)(share(summed.at[target], ping, target, elev).start)
+
+        @pl.when(rng > 0)
+        def _():
+            for target in range(DIRECT, ranks):
+                spill(summed.at[target], ping, target, elev).start()
 
     make_heads()
     for b in range(beams):
         make_beam(b)
-    for part, (start, some) in enumerate(zip(starts, PARTS)):
-        for b in range(0, beams, 2):
-            project(start, some, b)
-        project_edge(start, some)
-        if part == 0:
-            pl.semaphore_wait(barrier, ranks + jnp.where(rng > 0, ranks, 0))
-        swap_of(part).start()
-    for part in range(len(PARTS)):
-        swap_of(part).wait_recv()
-        combine(part)
-        send(part)
-
-    every = pl.ds(0, ranks - 1)
-    all_shares = pltpu.make_async_remote_copy(
-        src_ref=got.at[every],
-        dst_ref=got.at[every],
-        send_sem=share_send,
-        recv_sem=share_recv,
-        device_id={"elev": other},
-        device_id_type=MESH,
-    )
-    all_edges = pltpu.make_async_remote_copy(
-        src_ref=got_edge,
-        dst_ref=got_edge,
-        send_sem=edge_send,
-        recv_sem=edge_recv,
-        device_id={"elev": other},
-        device_id_type=MESH,
-    )
-
-    @pl.when(rng < groups - 1)
-    def _():
-        all_edges.wait_recv()
+    for b in range(0, beams, 2):
+        project(0, columns, b)
+    project_edge(0, columns)
+    pl.semaphore_wait(
+        barrier,
+        ranks - 1 + DIRECT + jnp.where(ping < DIRECT, 0, 1) + jnp.where(rng > 0, ranks + DIRECT, 0),
+    )
+    send_direct()
+    swap.start()
+    swap.wait_recv()
+    send_summed()
+
+    def shares_of(count):
+        return pltpu.make_async_remote_copy(
+            src_ref=got.at[pl.ds(0, count)],
+            dst_ref=got.at[pl.ds(0, count)],
+            send_sem=share_send,
+            recv_sem=share_recv,
+            device_id={"elev": other},
+            device_id_type=MESH,
+        )
+
+    def spills_of(count):
+        return pltpu.make_async_remote_copy(
+            src_ref=got_edge.at[pl.ds(0, count)],
+            dst_ref=got_edge.at[pl.ds(0, count)],
+            send_sem=edge_send,
+            recv_sem=edge_recv,
+            device_id={"elev": other},
+            device_id_type=MESH,
+        )
+
+    direct = ping < DIRECT
+    pl.when((rng < groups - 1) & direct)(spills_of(2 * ranks).wait_recv)
+    pl.when((rng < groups - 1) & (ping >= DIRECT))(spills_of(ranks).wait_recv)
 
     @pl.when(rng == groups - 1)
     def _():
         got_edge[...] = jnp.zeros_like(got_edge)
 
     edge = jnp.zeros((16, bins), F32)
-    for i in range(ranks):
-        edge = edge + got_edge[i].astype(F32)
+    for i in range(2 * ranks):
+        part = got_edge[i].astype(F32)
+        edge = edge + (part if i < ranks else jnp.where(direct, part, 0.0))
     edge = edge[:8]
-    got[ping] = summed[ping, pl.ds(0, 8 * beams), :]
-    all_shares.wait_recv()
+    got[jnp.where(direct, 2 * ping + elev, ping)] = summed[ping, pl.ds(0, 8 * beams), :]
+    pl.when(direct)(shares_of(2 * ranks - 1).wait_recv)
+    pl.when(ping >= DIRECT)(shares_of(ranks - 1).wait_recv)
     total = jnp.zeros((beams * 8, bins), F32)
-    for i in range(ranks):
-        total = total + got[i].astype(F32)
+    for i in range(2 * ranks):
+        part = got[i].astype(F32)
+        total = total + (part if i < ranks else jnp.where(direct, part, 0.0))
     for b in range(beams):
         moved = pltpu.roll(edge, (2 * bins - 8 - 16 * b) % bins, 1)
         end = jnp.where(lane >= bins - 8, moved, 0.0)
         result[:, b, :] = (total[8 * b : 8 * b + 8] + end) * scale
     out_ref[...] = result[...].astype(BF16)
 
-    all_shares.wait_send()
-    for part in range(len(PARTS)):
-        swap_of(part).wait_send()
-
-    @pl.when(rng > 0)
-    def _():
-        all_edges.wait_send()
+    shares_of(ranks - 1 + DIRECT).wait_send()
+    swap.wait_send()
+    pl.when(rng > 0)(spills_of(ranks + DIRECT).wait_send)
 
 
 def solution(mesh):
@@ -309,15 +346,15 @@
                 pltpu.VMEM((ranks, 2, beams * 8 + 16, bins), BF16),
                 pltpu.VMEM((ranks, beams * 8 + 16, bins), BF16),
                 pltpu.VMEM((ranks, beams * 8 + 16, bins), BF16),
-                pltpu.VMEM((ranks, beams * 8, bins), BF16),
-                pltpu.VMEM((ranks, 16, bins), BF16),
+                pltpu.VMEM((2 * ranks, beams * 8, bins), BF16),
+                pltpu.VMEM((2 * ranks, 16, bins), BF16),
                 pltpu.SemaphoreType.DMA((5,)),
                 pltpu.SemaphoreType.DMA,
                 pltpu.SemaphoreType.DMA,
                 pltpu.SemaphoreType.DMA,
                 pltpu.SemaphoreType.DMA,
-                pltpu.SemaphoreType.DMA((len(PARTS),)),
-                pltpu.SemaphoreType.DMA((len(PARTS),)),
+                pltpu.SemaphoreType.DMA,
+                pltpu.SemaphoreType.DMA,
             ],
             compiler_params=pltpu.CompilerParams(
                 collective_id=0, has_side_effects=True, vmem_limit_bytes=40 * 2**20

time: 12.9 us -> 12.4 us (0.961)
  Pallas kernels: 12.1 us -> 11.6 us
    pallas_call x1, Pallas kernels: 12.1 us -> 11.6 us  [body(): pl.pallas_call(functools.partial(kernel, scale, groups, ranks), out_shape...]
where the time goes in v8:
time: 12.4 us; the launch traced here: 12.2 us
  Pallas kernels  11.6 us (94%)
  local copies, waits for them, and re-layouts  0.61 us (5%)
    pallas_call x1, Pallas kernels, body(): pl.pallas_call(functools.partial(kernel, scale, groups, ranks), out_shape...  11.6 us
    unnamed x1, local copies, waits for them, and re-layouts  0.61 us

profile of v8, /device:TPU:1, one launch (start us, length us, event | category | flops | bytes accessed | tf_op | source)
XLA Modules:
  0.0 12.2 jit_solution(5522699935825371660)
XLA Ops:
  0.0 11.6 %shard_map.55 = bf16[8,8,128]{2,1,0:T(8,128)(2,1)S(1)} custom-call(bf16[4,8,64,128]{3,2,1,0:T(8,128)(2,1)} %echo_hbm.1, bf16[8,8,128]{2,1,0:T(8,128)(2,1)} %steer_hbm.1, s32[4]{0:T(128)} %off_hbm.1, s32[4,256]{1,0:T(4,128)} %delay_hbm.1, s32[4,128]{1,0:T(4,128)} %bitcast.1), custom_call_target="tpu_custom_call" | custom-call | flops 536870912 | bytes 524288 | tf_op jit(solution)/shard_map/pallas_call | solution.py:328
  11.6 0.6 %copy.7 = bf16[8,8,128]{2,1,0:T(8,128)(2,1)} copy(bf16[8,8,128]{2,1,0:T(8,128)(2,1)S(1)} %shard_map.55) | data formatting | bytes 32768

commit v9 on v8

--- a/solution.py
+++ b/solution.py
@@ -51,8 +51,15 @@
     ]
     for load in loads:
         load.start()
-    echo_load = pltpu.make_async_copy(echo_hbm, echo, small_sem.at[4])
-    echo_load.start()
+    each = pings // 2
+    echo_loads = [
+        pltpu.make_async_copy(
+            echo_hbm.at[pl.ds(i * each, each)], echo.at[pl.ds(i * each, each)], small_sem.at[4 + i]
+        )
+        for i in range(2)
+    ]
+    for load in echo_loads:
+        load.start()
 
     barrier = pltpu.get_barrier_semaphore()
     pl.semaphore_signal(
@@ -126,7 +133,19 @@
         moved = pltpu.roll(values, bins - count, 1)
         return jnp.where(lanes(values.shape) < bins - count, moved, jnp.zeros((), values.dtype))
 
-    echo_load.wait()
+    def beam_rows(p, b):
+        total = None
+        for e in range(elems):
+            line = jnp.concatenate([spread[b, e]] * (along // 8), axis=0)
+            term = echo[p, e].astype(F32) * line
+            total = term if total is None else total + term
+        return total.astype(BF16)
+
+    beam_parts = [[] for _ in range(beams)]
+    for i, load in enumerate(echo_loads):
+        load.wait()
+        for b in range(beams):
+            beam_parts[b] += [beam_rows(p, b) for p in range(i * each, (i + 1) * each)]
 
     store = {}
 
@@ -156,15 +175,7 @@
             RHS(beams, low)[...] = moved
 
     def make_beam(b):
-        rows = []
-        for p in range(pings):
-            total = None
-            for e in range(elems):
-                line = jnp.concatenate([spread[b, e]] * (along // 8), axis=0)
-                term = echo[p, e].astype(F32) * line
-                total = term if total is None else total + term
-            rows.append(total.astype(BF16))
-        beam = jnp.concatenate(rows, axis=0)
+        beam = jnp.concatenate(beam_parts[b], axis=0)
         RHS(b, 0)[...] = beam
         for low in range(1, 4):
             RHS(b, low)[...] = later(beam, low)
@@ -257,8 +268,8 @@
         barrier,
         ranks - 1 + DIRECT + jnp.where(ping < DIRECT, 0, 1) + jnp.where(rng > 0, ranks + DIRECT, 0),
     )
+    swap.start()
     send_direct()
-    swap.start()
     swap.wait_recv()
     send_summed()
 
@@ -348,7 +359,7 @@
                 pltpu.VMEM((ranks, beams * 8 + 16, bins), BF16),
                 pltpu.VMEM((2 * ranks, beams * 8, bins), BF16),
                 pltpu.VMEM((2 * ranks, 16, bins), BF16),
-                pltpu.SemaphoreType.DMA((5,)),
+                pltpu.SemaphoreType.DMA((6,)),
                 pltpu.SemaphoreType.DMA,
                 pltpu.SemaphoreType.DMA,
                 pltpu.SemaphoreType.DMA,

time: 12.4 us -> 12.4 us (level)
  no operation moved by 1% of the time
where the time goes in v9:
time: 12.4 us; the launch traced here: 12.2 us
  Pallas kernels  11.6 us (94%)
  local copies, waits for them, and re-layouts  0.61 us (5%)
    pallas_call x1, Pallas kernels, body(): pl.pallas_call(functools.partial(kernel, scale, groups, ranks), out_shape...  11.6 us
    unnamed x1, local copies, waits for them, and re-layouts  0.61 us

profile of v9, /device:TPU:1, one launch (start us, length us, event | category | flops | bytes accessed | tf_op | source)
XLA Modules:
  0.0 12.2 jit_solution(927960629560784188)
XLA Ops:
  0.0 11.6 %shard_map.55 = bf16[8,8,128]{2,1,0:T(8,128)(2,1)S(1)} custom-call(bf16[4,8,64,128]{3,2,1,0:T(8,128)(2,1)} %echo_hbm.1, bf16[8,8,128]{2,1,0:T(8,128)(2,1)} %steer_hbm.1, s32[4]{0:T(128)} %off_hbm.1, s32[4,256]{1,0:T(4,128)} %delay_hbm.1, s32[4,128]{1,0:T(4,128)} %bitcast.1), custom_call_target="tpu_custom_call" | custom-call | flops 536870912 | bytes 524288 | tf_op jit(solution)/shard_map/pallas_call | solution.py:339
  11.6 0.6 %copy.7 = bf16[8,8,128]{2,1,0:T(8,128)(2,1)} copy(bf16[8,8,128]{2,1,0:T(8,128)(2,1)S(1)} %shard_map.55) | data formatting | bytes 32768

commit v10 on v9

--- a/solution.py
+++ b/solution.py
@@ -43,6 +43,39 @@
     beams = steer.shape[1]
     depth = pings * along
 
+    barrier = pltpu.get_barrier_semaphore()
+    pl.semaphore_signal(
+        barrier, inc=1, device_id={"elev": other}, device_id_type=MESH
+    )
+    for route in ROUTES[:-1]:
+        pl.semaphore_signal(
+            barrier, inc=1, device_id={"ping": target_of(ping, route)}, device_id_type=MESH
+        )
+
+    @pl.when(ping < DIRECT)
+    def _():
+        for route in ROUTES[:-1]:
+            pl.semaphore_signal(
+                barrier, inc=1, device_id_type=MESH,
+                device_id={"ping": target_of(ping, route), "elev": other},
+            )
+
+    @pl.when(rng < groups - 1)
+    def _():
+        for route in ROUTES:
+            pl.semaphore_signal(
+                barrier, inc=1, device_id_type=MESH,
+                device_id={"ping": target_of(ping, route), "range": rng + 1},
+            )
+
+    @pl.when((rng < groups - 1) & (ping < DIRECT))
+    def _():
+        for route in ROUTES:
+            pl.semaphore_signal(
+                barrier, inc=1, device_id_type=MESH,
+                device_id={"ping": target_of(ping, route), "range": rng + 1, "elev": other},
+            )
+
     loads = [
         pltpu.make_async_copy(src, dst, small_sem.at[i])
         for i, (src, dst) in enumerate(
@@ -60,39 +93,6 @@
     ]
     for load in echo_loads:
         load.start()
-
-    barrier = pltpu.get_barrier_semaphore()
-    pl.semaphore_signal(
-        barrier, inc=1, device_id={"elev": other}, device_id_type=MESH
-    )
-    for route in ROUTES[:-1]:
-        pl.semaphore_signal(
-            barrier, inc=1, device_id={"ping": target_of(ping, route)}, device_id_type=MESH
-        )
-
-    @pl.when(ping < DIRECT)
-    def _():
-        for route in ROUTES[:-1]:
-            pl.semaphore_signal(
-                barrier, inc=1, device_id_type=MESH,
-                device_id={"ping": target_of(ping, route), "elev": other},
-            )
-
-    @pl.when(rng < groups - 1)
-    def _():
-        for route in ROUTES:
-            pl.semaphore_signal(
-                barrier, inc=1, device_id_type=MESH,
-                device_id={"ping": target_of(ping, route), "range": rng + 1},
-            )
-
-    @pl.when((rng < groups - 1) & (ping < DIRECT))
-    def _():
-        for route in ROUTES:
-            pl.semaphore_signal(
-                barrier, inc=1, device_id_type=MESH,
-                device_id={"ping": target_of(ping, route), "range": rng + 1, "elev": other},
-            )
 
     for load in loads:
         load.wait()

time: 12.4 us -> 12.4 us (level)
  no operation moved by 1% of the time
where the time goes in v10:
time: 12.4 us; the launch traced here: 12.2 us
  Pallas kernels  11.6 us (94%)
  local copies, waits for them, and re-layouts  0.61 us (5%)
    pallas_call x1, Pallas kernels, body(): pl.pallas_call(functools.partial(kernel, scale, groups, ranks), out_shape...  11.6 us
    unnamed x1, local copies, waits for them, and re-layouts  0.61 us

profile of v10, /device:TPU:1, one launch (start us, length us, event | category | flops | bytes accessed | tf_op | source)
XLA Modules:
  0.0 12.2 jit_solution(13184168765920708444)
XLA Ops:
  0.0 11.6 %shard_map.55 = bf16[8,8,128]{2,1,0:T(8,128)(2,1)S(1)} custom-call(bf16[4,8,64,128]{3,2,1,0:T(8,128)(2,1)} %echo_hbm.1, bf16[8,8,128]{2,1,0:T(8,128)(2,1)} %steer_hbm.1, s32[4]{0:T(128)} %off_hbm.1, s32[4,256]{1,0:T(4,128)} %delay_hbm.1, s32[4,128]{1,0:T(4,128)} %bitcast.1), custom_call_target="tpu_custom_call" | custom-call | flops 536870912 | bytes 524288 | tf_op jit(solution)/shard_map/pallas_call | solution.py:339
  11.6 0.6 %copy.7 = bf16[8,8,128]{2,1,0:T(8,128)(2,1)} copy(bf16[8,8,128]{2,1,0:T(8,128)(2,1)S(1)} %shard_map.55) | data formatting | bytes 32768

commit v11 on v10

--- a/solution.py
+++ b/solution.py
@@ -82,8 +82,6 @@
             ((steer_hbm, steer), (delay_hbm, delay), (off_hbm, off), (ap_hbm, ap))
         )
     ]
-    for load in loads:
-        load.start()
     each = pings // 2
     echo_loads = [
         pltpu.make_async_copy(
@@ -92,6 +90,8 @@
         for i in range(2)
     ]
     for load in echo_loads:
+        load.start()
+    for load in loads:
         load.start()
 
     for load in loads:

time: 12.4 us -> 12.4 us (level)
  no operation moved by 1% of the time
where the time goes in v11:
time: 12.4 us; the launch traced here: 12.2 us
  Pallas kernels  11.6 us (94%)
  local copies, waits for them, and re-layouts  0.61 us (5%)
    pallas_call x1, Pallas kernels, body(): pl.pallas_call(functools.partial(kernel, scale, groups, ranks), out_shape...  11.6 us
    unnamed x1, local copies, waits for them, and re-layouts  0.61 us

profile of v11, /device:TPU:1, one launch (start us, length us, event | category | flops | bytes accessed | tf_op | source)
XLA Modules:
  0.0 12.2 jit_solution(13152131970352522354)
XLA Ops:
  0.0 11.6 %shard_map.55 = bf16[8,8,128]{2,1,0:T(8,128)(2,1)S(1)} custom-call(bf16[4,8,64,128]{3,2,1,0:T(8,128)(2,1)} %echo_hbm.1, bf16[8,8,128]{2,1,0:T(8,128)(2,1)} %steer_hbm.1, s32[4]{0:T(128)} %off_hbm.1, s32[4,256]{1,0:T(4,128)} %delay_hbm.1, s32[4,128]{1,0:T(4,128)} %bitcast.1), custom_call_target="tpu_custom_call" | custom-call | flops 536870912 | bytes 524288 | tf_op jit(solution)/shard_map/pallas_call | solution.py:339
  11.6 0.6 %copy.7 = bf16[8,8,128]{2,1,0:T(8,128)(2,1)} copy(bf16[8,8,128]{2,1,0:T(8,128)(2,1)S(1)} %shard_map.55) | data formatting | bytes 32768
